TPU v7x, 32 devices: a whole 2x2x4 slice. The times are simulated.
32 devices in a mesh: section: 2 (over core), dp: 16 (over z, y, x).
Axes of the slice: x: 2, y: 2, z: 4, core: 2. Of those that a mesh axis runs over, the one named last changes fastest.
Arguments:
- inputs: bfloat16 [2, 1, 128, 128, 512], P(None, None, 'dp'), may hold values from -64 to 64
- cotangent: bfloat16 [2, 1, 128, 128, 512], P(None, None, 'dp'), may hold values from -6 to 6
- shapes: int32 [2, 2], replicated, may hold values from 96 to 128, as said below
- local_to_local: bfloat16 [2, 2, 9, 128, 128], P('section'), may hold values from -0.09375 to 0.09375
- global_to_local: bfloat16 [2, 2, 9, 384, 128], P('section'), may hold values from -0.09375 to 0.09375
- local_to_global: bfloat16 [2, 2, 9, 128, 384], P('section'), may hold values from -0.1875 to 0.1875
- spec_reduce: bfloat16 [2, 2, 384, 192], P('section'), may hold values from -0.3125 to 0.3125
- spec_mix: bfloat16 [2, 2, 384, 384], P('section'), may hold values from -0.3125 to 0.3125
- spec_expand: bfloat16 [2, 2, 192, 384], P('section'), may hold values from -0.4375 to 0.4375
- norm_gains: float32 [2, 2, 1088], P('section'), may hold values from 0.1 to 1.9
- norm_biases: float32 [2, 2, 1088], P('section'), may hold values from -3 to 3
- run_means: float32 [2, 2, 1088], P('section'), may hold values from -3 to 3
- run_vars: float32 [2, 2, 1088], P('section'), may hold values from 0.5 to 2
Outputs:
- block_outputs: bfloat16 [2, 2, 1, 128, 128, 512], P('section', None, None, 'dp')
- input_grads: float32 [2, 2, 1, 128, 128, 512], P('section', None, None, 'dp')
- grad_local_to_local: float32 [2, 2, 9, 128, 128], P('section')
- grad_global_to_local: float32 [2, 2, 9, 384, 128], P('section')
- grad_local_to_global: float32 [2, 2, 9, 128, 384], P('section')
- grad_spec_reduce: float32 [2, 2, 384, 192], P('section')
- grad_spec_mix: float32 [2, 2, 384, 384], P('section')
- grad_spec_expand: float32 [2, 2, 192, 384], P('section')
- grad_gains: float32 [2, 2, 1088], P('section')
- grad_biases: float32 [2, 2, 1088], P('section')
- new_means: float32 [2, 2, 1088], P('section')
- new_vars: float32 [2, 2, 1088], P('section')
Inputs may be any that keep to these rules, and one draw needn't show every extreme that they name: `shapes`: each row is (height, width) of all maps of a micro-batch, both multiples of 8; some micro-batch has height 128.
All inputs are finite; a program needn't handle non-finite values.
Results may differ from a plain program's by a relative error of at most 0.025.
Values may be sent and summed in bfloat16 or wider, within the bound.
A program may use at most 256 MiB of HBM per device.

v0:
```python
import jax
import jax.numpy as jnp
from jax import lax
from jax.sharding import PartitionSpec as P

CL = 128
CG = 384
CS = 192
LONG = 128


EPSILON = 1e-05
MOMENTUM = 0.1
PRECISE = lax.Precision.HIGHEST


def with_halo(block, sides, width):
    for axis, dim in sides:
        count = lax.axis_size(axis)
        forward = [(i, i + 1) for i in range(count - 1)]
        backward = [(target, source) for source, target in forward]
        low = lax.ppermute(
            lax.slice_in_dim(block, block.shape[dim] - width, None, axis=dim), axis, forward
        )
        high = lax.ppermute(lax.slice_in_dim(block, 0, width, axis=dim), axis, backward)
        block = jnp.concatenate([low, block, high], axis=dim)
    return block


def from_behind(value, axis, steps):
    count = lax.axis_size(axis)
    first, last = (max(0, -steps), min(count, count - steps))
    return lax.ppermute(value, axis, [(source, source + steps) for source in range(first, last)])


def dft_tables(height, width, long_side, freq_total):
    position = jnp.arange(long_side, dtype=jnp.int32)
    frequency = jnp.arange(freq_total, dtype=jnp.int32)
    half_width = width // 2
    width_real = width.astype(jnp.float32)
    height_real = height.astype(jnp.float32)
    width_phase = position[:, None] * frequency[None, :] % width
    width_angle = 2.0 * jnp.pi / width_real * width_phase.astype(jnp.float32)
    width_valid = ((position[:, None] < width) & (frequency[None, :] <= half_width)).astype(
        jnp.float32
    )
    width_scale = lax.rsqrt(width_real)
    fwd_cos = jnp.cos(width_angle) * width_scale * width_valid
    fwd_sin = -jnp.sin(width_angle) * width_scale * width_valid
    edge_freq = (frequency == 0) | (frequency == half_width)
    freq_weight = jnp.where(edge_freq, 1.0, 2.0).astype(jnp.float32)
    inv_cos = freq_weight[:, None] * fwd_cos.T
    inv_sin = freq_weight[:, None] * fwd_sin.T
    height_phase = position[:, None] * position[None, :] % height
    height_angle = 2.0 * jnp.pi / height_real * height_phase.astype(jnp.float32)
    height_valid = ((position[:, None] < height) & (position[None, :] < height)).astype(jnp.float32)
    height_scale = lax.rsqrt(height_real)
    row_cos = jnp.cos(height_angle) * height_scale * height_valid
    row_sin = jnp.sin(height_angle) * height_scale * height_valid
    return (fwd_cos, fwd_sin, inv_cos, inv_sin, row_cos, row_sin)


def geometry(shape_row, band_index, band_size, freq_total, freq_local, map_count):
    height = shape_row[0]
    width = shape_row[1]
    position = jnp.arange(LONG, dtype=jnp.int32)
    band_rows = band_index * band_size + jnp.arange(band_size, dtype=jnp.int32)
    pix_mask = ((band_rows[:, None] < height) & (position[None, :] < width)).astype(jnp.float32)[
        None, :, :, None
    ]
    local_freq = band_index * freq_local + jnp.arange(freq_local, dtype=jnp.int32)
    freq_mask = ((position[:, None] < height) & (local_freq[None, :] <= width // 2)).astype(
        jnp.float32
    )[None, :, :, None]
    pix_count = (map_count * height * width).astype(jnp.float32)
    spec_count = (map_count * height * (width // 2 + 1)).astype(jnp.float32)
    return (pix_mask, freq_mask, pix_count, spec_count, dft_tables(height, width, LONG, freq_total))


def conv_rows(padded, kernel):
    shaped = kernel.reshape(3, 3, kernel.shape[1], kernel.shape[2])
    return lax.conv_general_dilated(
        padded,
        shaped,
        (1, 1),
        "VALID",
        dimension_numbers=("NHWC", "HWIO", "NHWC"),
        preferred_element_type=jnp.float32,
    )


def flipped(kernel):
    shaped = kernel.reshape(3, 3, kernel.shape[1], kernel.shape[2])[::-1, ::-1]
    return jnp.swapaxes(shaped, 2, 3).reshape(9, kernel.shape[2], kernel.shape[1])


def kernel_grad(padded, grad_out, band_size, width):
    tap_grads = []
    for row_tap in range(3):
        for col_tap in range(3):
            window = padded[:, row_tap : row_tap + band_size, col_tap : col_tap + width, :]
            tap_grads.append(
                jnp.einsum("mrwi,mrwo->io", window, grad_out, preferred_element_type=jnp.float32)
            )
    return jnp.stack(tap_grads)


def width_forward(entry, table):
    return jnp.einsum("mrwc,wf->mrfc", entry, table, precision=PRECISE)


def width_forward_adj(entry, table):
    return jnp.einsum("mrfc,wf->mrwc", entry, table, precision=PRECISE)


def width_inverse(entry, table):
    return jnp.einsum("mrfc,fw->mrwc", entry, table, precision=PRECISE)


def width_inverse_adj(entry, table):
    return jnp.einsum("mrwc,fw->mrfc", entry, table, precision=PRECISE)


def height_apply(table, entry):
    return jnp.einsum("kn,mnfc->mkfc", table, entry, precision=PRECISE)


def height_adjoint(table, entry):
    return jnp.einsum("kn,mkfc->mnfc", table, entry, precision=PRECISE)


def rows_forward(row_cos, row_sin, entry):
    half_ch = entry.shape[-1] // 2
    real_in = entry[..., :half_ch]
    imag_in = entry[..., half_ch:]
    real_out = height_apply(row_cos, real_in) + height_apply(row_sin, imag_in)
    imag_out = height_apply(row_cos, imag_in) - height_apply(row_sin, real_in)
    return jnp.concatenate([real_out, imag_out], axis=-1)


def rows_inverse(row_cos, row_sin, entry):
    half_ch = entry.shape[-1] // 2
    real_in = entry[..., :half_ch]
    imag_in = entry[..., half_ch:]
    real_out = height_adjoint(row_cos, real_in) - height_adjoint(row_sin, imag_in)
    imag_out = height_adjoint(row_cos, imag_in) + height_adjoint(row_sin, real_in)
    return jnp.concatenate([real_out, imag_out], axis=-1)


def split_pairs(totals, widths):
    pairs = []
    offset = 0
    for lead_width, tail_width in zip(widths[0::2], widths[1::2]):
        lead_part = totals[offset : offset + lead_width]
        tail_part = totals[offset + lead_width : offset + lead_width + tail_width]
        pairs.append((lead_part, tail_part))
        offset = offset + lead_width + tail_width
    return pairs


def moments(entries, weights):
    pieces = []
    for entry, weight in zip(entries, weights):
        masked = entry * weight
        pieces.append(jnp.sum(masked, axis=(0, 1, 2)))
        pieces.append(jnp.sum(masked * entry, axis=(0, 1, 2)))
    totals = lax.psum(jnp.concatenate(pieces), "dp")
    return split_pairs(totals, [piece.shape[0] for piece in pieces])


def grad_moments(grads_in, normed_in):
    pieces = []
    for grad_pre, normed in zip(grads_in, normed_in):
        pieces.append(jnp.sum(grad_pre, axis=(0, 1, 2)))
        pieces.append(jnp.sum(grad_pre * normed, axis=(0, 1, 2)))
    totals = lax.psum(jnp.concatenate(pieces), "dp")
    return split_pairs(totals, [piece.shape[0] for piece in pieces])


def normalize(entry, sum_pair, count_now):
    mean_val = sum_pair[0] / count_now
    var_val = sum_pair[1] / count_now - mean_val * mean_val
    inv_std = lax.rsqrt(var_val + EPSILON)
    return ((entry - mean_val) * inv_std, inv_std, mean_val, var_val)


def silu_slope(pre_act):
    sigmoid_val = jax.nn.sigmoid(pre_act)
    return sigmoid_val * (1.0 + pre_act * (1.0 - sigmoid_val))


def norm_backward(grad_pre, normed, inv_std, gain_part, sum_pair, count_now, weight):
    return (
        weight
        * inv_std
        * gain_part
        * (grad_pre - sum_pair[0] / count_now - normed * sum_pair[1] / count_now)
    )


def layer_forward(layer_in, geometry_now, kernels, gain_vec, bias_vec):
    pix_mask, freq_mask, pix_count, spec_count, tables = geometry_now
    fwd_cos, fwd_sin, inv_cos, inv_sin, row_cos, row_sin = tables
    local_kernel, lift_kernel, reduce_kernel, mix_kernel, expand_kernel = kernels
    acts_low = layer_in.astype(jnp.bfloat16)
    padded = with_halo(acts_low, (("dp", 1),), 1)
    padded = jnp.pad(padded, ((0, 0), (0, 0), (1, 1), (0, 0)))
    local_out = conv_rows(padded, local_kernel)
    global_conv = conv_rows(padded[..., :CL], lift_kernel)
    reduced = jnp.einsum(
        "mrwc,cd->mrwd", acts_low[..., CL:], reduce_kernel, preferred_element_type=jnp.float32
    )
    one_stats = moments([reduced], [pix_mask])[0]
    normed_one, inv_one, mean_one, var_one = normalize(reduced, one_stats, pix_count)
    pre_one = normed_one * gain_vec[:CS] + bias_vec[:CS]
    upper_spec = jax.nn.silu(pre_one) * pix_mask
    spectrum = jnp.concatenate(
        [width_forward(upper_spec, fwd_cos), width_forward(upper_spec, fwd_sin)], axis=-1
    ).astype(jnp.bfloat16)
    columns = lax.all_to_all(spectrum, "dp", split_axis=2, concat_axis=1, tiled=True).astype(
        jnp.float32
    )
    spectra = rows_forward(row_cos, row_sin, columns).astype(jnp.bfloat16)
    mixed = jnp.einsum("mkfc,cd->mkfd", spectra, mix_kernel, preferred_element_type=jnp.float32)
    two_stats = moments([mixed], [freq_mask])[0]
    normed_two, inv_two, mean_two, var_two = normalize(mixed, two_stats, spec_count)
    pre_two = normed_two * gain_vec[CS : 3 * CS] + bias_vec[CS : 3 * CS]
    activated = jax.nn.silu(pre_two) * freq_mask
    inverse = rows_inverse(row_cos, row_sin, activated).astype(jnp.bfloat16)
    returned = lax.all_to_all(inverse, "dp", split_axis=1, concat_axis=2, tiled=True).astype(
        jnp.float32
    )
    half_ch = returned.shape[-1] // 2
    restored = width_inverse(returned[..., :half_ch], inv_cos) + width_inverse(
        returned[..., half_ch:], inv_sin
    )
    summed = (upper_spec + restored).astype(jnp.bfloat16)
    spec_out = jnp.einsum(
        "mrwc,cd->mrwd", summed, expand_kernel, preferred_element_type=jnp.float32
    )
    global_out = global_conv + spec_out
    loc_stats, glo_stats = moments([local_out, global_out], [pix_mask, pix_mask])
    normed_loc, inv_loc, mean_loc, var_loc = normalize(local_out, loc_stats, pix_count)
    normed_glo, inv_glo, mean_glo, var_glo = normalize(global_out, glo_stats, pix_count)
    pre_loc = normed_loc * gain_vec[3 * CS : 3 * CS + CL] + bias_vec[3 * CS : 3 * CS + CL]
    pre_glo = normed_glo * gain_vec[3 * CS + CL :] + bias_vec[3 * CS + CL :]
    result = jnp.concatenate([jax.nn.silu(pre_loc), jax.nn.silu(pre_glo)], axis=-1) * pix_mask
    stored = (
        padded,
        pre_one,
        normed_one,
        inv_one,
        spectra,
        pre_two,
        normed_two,
        inv_two,
        summed,
        pre_loc,
        normed_loc,
        inv_loc,
        pre_glo,
        normed_glo,
        inv_glo,
    )
    means_layer = jnp.concatenate([mean_one, mean_two, mean_loc, mean_glo])
    vars_layer = jnp.concatenate([var_one, var_two, var_loc, var_glo])
    return (result, stored, (means_layer, vars_layer))


def layer_backward(grad_result, stored, geometry_now, kernels, gain_vec):
    (
        padded,
        pre_one,
        normed_one,
        inv_one,
        spectra,
        pre_two,
        normed_two,
        inv_two,
        summed,
        pre_loc,
        normed_loc,
        inv_loc,
        pre_glo,
        normed_glo,
        inv_glo,
    ) = stored
    pix_mask, freq_mask, pix_count, spec_count, tables = geometry_now
    fwd_cos, fwd_sin, inv_cos, inv_sin, row_cos, row_sin = tables
    local_kernel, lift_kernel, reduce_kernel, mix_kernel, expand_kernel = kernels
    band_size = pre_one.shape[1]
    width = pre_one.shape[2]
    grad_loc = grad_result[..., :CL] * pix_mask * silu_slope(pre_loc)
    grad_glo = grad_result[..., CL:] * pix_mask * silu_slope(pre_glo)
    loc_pair, glo_pair = grad_moments([grad_loc, grad_glo], [normed_loc, normed_glo])
    d_local = norm_backward(
        grad_loc, normed_loc, inv_loc, gain_vec[3 * CS : 3 * CS + CL], loc_pair, pix_count, pix_mask
    ).astype(jnp.bfloat16)
    d_global = norm_backward(
        grad_glo, normed_glo, inv_glo, gain_vec[3 * CS + CL :], glo_pair, pix_count, pix_mask
    ).astype(jnp.bfloat16)
    grad_expand = jnp.einsum("mrwc,mrwd->cd", summed, d_global, preferred_element_type=jnp.float32)
    d_summed = jnp.einsum(
        "mrwd,cd->mrwc", d_global, expand_kernel, preferred_element_type=jnp.float32
    )
    d_returned = jnp.concatenate(
        [width_inverse_adj(d_summed, inv_cos), width_inverse_adj(d_summed, inv_sin)], axis=-1
    ).astype(jnp.bfloat16)
    d_inverse = lax.all_to_all(d_returned, "dp", split_axis=2, concat_axis=1, tiled=True).astype(
        jnp.float32
    )
    d_activated = rows_forward(row_cos, row_sin, d_inverse)
    grad_two = d_activated * freq_mask * silu_slope(pre_two)
    two_pair = grad_moments([grad_two], [normed_two])[0]
    d_mixed = norm_backward(
        grad_two, normed_two, inv_two, gain_vec[CS : 3 * CS], two_pair, spec_count, freq_mask
    ).astype(jnp.bfloat16)
    grad_mix = jnp.einsum("mkfc,mkfd->cd", spectra, d_mixed, preferred_element_type=jnp.float32)
    d_spectra = jnp.einsum("mkfd,cd->mkfc", d_mixed, mix_kernel, preferred_element_type=jnp.float32)
    d_columns = rows_inverse(row_cos, row_sin, d_spectra).astype(jnp.bfloat16)
    d_spectrum = lax.all_to_all(d_columns, "dp", split_axis=1, concat_axis=2, tiled=True).astype(
        jnp.float32
    )
    half_ch = d_spectrum.shape[-1] // 2
    d_upper = (
        d_summed
        + width_forward_adj(d_spectrum[..., :half_ch], fwd_cos)
        + width_forward_adj(d_spectrum[..., half_ch:], fwd_sin)
    )
    grad_one = d_upper * pix_mask * silu_slope(pre_one)
    one_pair = grad_moments([grad_one], [normed_one])[0]
    d_reduced = norm_backward(
        grad_one, normed_one, inv_one, gain_vec[:CS], one_pair, pix_count, pix_mask
    ).astype(jnp.bfloat16)
    acts_low = padded[:, 1:-1, 1:-1, :]
    grad_reduce = jnp.einsum(
        "mrwc,mrwd->cd", acts_low[..., CL:], d_reduced, preferred_element_type=jnp.float32
    )
    d_global_in = jnp.einsum(
        "mrwd,cd->mrwc", d_reduced, reduce_kernel, preferred_element_type=jnp.float32
    )
    grad_outs = jnp.concatenate([d_local, d_global], axis=-1)
    grad_pad = with_halo(grad_outs, (("dp", 1),), 1)
    grad_pad = jnp.pad(grad_pad, ((0, 0), (0, 0), (1, 1), (0, 0)))
    d_acts = conv_rows(grad_pad[..., :CL], flipped(local_kernel))
    d_lift = conv_rows(grad_pad[..., CL:], flipped(lift_kernel))
    d_input = d_acts + jnp.concatenate([d_lift, d_global_in], axis=-1)
    grad_local_kernel = kernel_grad(padded, d_local, band_size, width)
    grad_lift = kernel_grad(padded[..., :CL], d_global, band_size, width)
    gains_grad = jnp.concatenate([one_pair[1], two_pair[1], loc_pair[1], glo_pair[1]])
    biases_grad = jnp.concatenate([one_pair[0], two_pair[0], loc_pair[0], glo_pair[0]])
    return (
        d_input,
        (grad_local_kernel, grad_lift, grad_reduce, grad_mix, grad_expand),
        (gains_grad, biases_grad),
    )


def block_forward(block_in, geometry_now, kernels, gain_all, bias_all):
    base = block_in.astype(jnp.float32) * geometry_now[0]
    first_out, first_stored, first_stats = layer_forward(
        base, geometry_now, kernels[0], gain_all[0], bias_all[0]
    )
    second_out, second_stored, second_stats = layer_forward(
        first_out, geometry_now, kernels[1], gain_all[1], bias_all[1]
    )
    return (
        (second_out + base).astype(jnp.bfloat16),
        (first_stored, second_stored),
        (first_stats, second_stats),
    )


def block_backward(grad_in, stored, geometry_now, kernels, gain_all):
    pix_mask = geometry_now[0]
    grad_masked = grad_in * pix_mask
    d_first, second_kernels, second_norms = layer_backward(
        grad_masked, stored[1], geometry_now, kernels[1], gain_all[1]
    )
    d_base, first_kernels, first_norms = layer_backward(
        d_first, stored[0], geometry_now, kernels[0], gain_all[0]
    )
    return (
        (grad_masked + d_base) * pix_mask,
        (first_kernels, second_kernels),
        (first_norms, second_norms),
    )


def running_update(mean_now, var_now, layer_stats, geometry_now):
    pix_count = geometry_now[2]
    spec_count = geometry_now[3]
    counts = jnp.concatenate(
        [
            jnp.full((CS,), pix_count, jnp.float32),
            jnp.full((2 * CS,), spec_count, jnp.float32),
            jnp.full((CL + CG,), pix_count, jnp.float32),
        ]
    )
    batch_means = jnp.stack([layer_stats[0][0], layer_stats[1][0]])
    batch_vars = jnp.stack([layer_stats[0][1], layer_stats[1][1]])
    new_mean = (1.0 - MOMENTUM) * mean_now + MOMENTUM * batch_means
    new_var = (1.0 - MOMENTUM) * var_now + MOMENTUM * batch_vars * counts / (counts - 1.0)
    return (new_mean, new_var)


def on_device(
    inputs,
    cotangent,
    shapes,
    local_to_local,
    global_to_local,
    local_to_global,
    spec_reduce,
    spec_mix,
    spec_expand,
    norm_gains,
    norm_biases,
    run_means,
    run_vars,
):
    section_id = lax.axis_index("section")
    band_index = lax.axis_index("dp")
    n_dp = lax.axis_size("dp")
    micro_count = inputs.shape[0]
    map_count = inputs.shape[1]
    band_size = inputs.shape[2]
    freq_total = (LONG // 2 + n_dp) // n_dp * n_dp
    freq_local = freq_total // n_dp
    kernels = []
    for layer_pos in range(2):
        local_kernel = jnp.concatenate(
            [local_to_local[0, layer_pos], global_to_local[0, layer_pos]], axis=1
        )
        kernels.append(
            (
                local_kernel,
                local_to_global[0, layer_pos],
                spec_reduce[0, layer_pos],
                spec_mix[0, layer_pos],
                spec_expand[0, layer_pos],
            )
        )
    gain_all = norm_gains[0]
    bias_all = norm_biases[0]
    received = jnp.zeros(inputs.shape[1:], jnp.bfloat16)
    run_mean = run_means[0]
    run_var = run_vars[0]
    outputs = jnp.zeros(inputs.shape, jnp.bfloat16)
    saved_inputs = []
    saved_geometry = []
    for tick_pos in range(micro_count + 1):
        micro_index = tick_pos - section_id
        is_valid = (micro_index >= 0) & (micro_index < micro_count)
        micro_slot = jnp.clip(micro_index, 0, micro_count - 1)
        own_input = lax.dynamic_index_in_dim(inputs, micro_slot, 0, keepdims=False)
        block_in = jnp.where(section_id == 0, own_input, received)
        shape_row = lax.dynamic_index_in_dim(shapes, micro_slot, 0, keepdims=False)
        geometry_now = geometry(shape_row, band_index, band_size, freq_total, freq_local, map_count)
        block_out, stored, layer_stats = block_forward(
            block_in, geometry_now, kernels, gain_all, bias_all
        )
        new_mean, new_var = running_update(run_mean, run_var, layer_stats, geometry_now)
        run_mean = jnp.where(is_valid, new_mean, run_mean)
        run_var = jnp.where(is_valid, new_var, run_var)
        updated = lax.dynamic_update_index_in_dim(outputs, block_out, micro_slot, 0)
        outputs = jnp.where(is_valid, updated, outputs)
        saved_inputs.append(block_in)
        saved_geometry.append(geometry_now)
        if tick_pos < micro_count:
            received = from_behind(block_out, "section", 1)
    kernel_acc = [jnp.zeros((2,) + part_now.shape, jnp.float32) for part_now in kernels[0]]
    gain_acc = jnp.zeros(gain_all.shape, jnp.float32)
    bias_acc = jnp.zeros(bias_all.shape, jnp.float32)
    received_grad = jnp.zeros(inputs.shape[1:], jnp.bfloat16)
    grads_out = jnp.zeros(inputs.shape, jnp.float32)
    for tick_pos in range(micro_count + 1):
        micro_index = micro_count - tick_pos - section_id
        is_valid = (micro_index >= 0) & (micro_index < micro_count)
        micro_slot = jnp.clip(micro_index, 0, micro_count - 1)
        scale_valid = is_valid.astype(jnp.float32)
        forward_tick = micro_count - tick_pos
        geometry_now = saved_geometry[forward_tick]
        recomputed = block_forward(
            saved_inputs[forward_tick], geometry_now, kernels, gain_all, bias_all
        )
        stored = recomputed[1]
        own_grad = lax.dynamic_index_in_dim(cotangent, micro_slot, 0, keepdims=False)
        grad_in = jnp.where(section_id == 1, own_grad, received_grad).astype(jnp.float32)
        grad_input, kernel_grads, norm_grads = block_backward(
            grad_in, stored, geometry_now, kernels, gain_all
        )
        sent_grad = grad_input.astype(jnp.bfloat16)
        kept_grad = jnp.where(section_id == 1, sent_grad.astype(jnp.float32), grad_input)
        updated = lax.dynamic_update_index_in_dim(grads_out, kept_grad, micro_slot, 0)
        grads_out = jnp.where(is_valid, updated, grads_out)
        stacked = [
            jnp.stack([kernel_grads[0][part_pos], kernel_grads[1][part_pos]]) * scale_valid
            for part_pos in range(5)
        ]
        gain_acc = gain_acc + jnp.stack([norm_grads[0][0], norm_grads[1][0]]) * scale_valid
        bias_acc = bias_acc + jnp.stack([norm_grads[0][1], norm_grads[1][1]]) * scale_valid
        kernel_acc = [acc_part + new_part for acc_part, new_part in zip(kernel_acc, stacked)]
        if tick_pos < micro_count:
            received_grad = from_behind(sent_grad, "section", -1)
    totals = lax.psum(
        (kernel_acc[0], kernel_acc[1], kernel_acc[2], kernel_acc[3], kernel_acc[4]), "dp"
    )
    grad_ll = totals[0][:, :, :CL, :]
    grad_gl = totals[0][:, :, CL:, :]
    return (
        outputs[None],
        grads_out[None],
        grad_ll[None],
        grad_gl[None],
        totals[1][None],
        totals[2][None],
        totals[3][None],
        totals[4][None],
        gain_acc[None],
        bias_acc[None],
        run_mean[None],
        run_var[None],
    )


def solution(mesh):
    in_specs = (
        P(None, None, "dp", None, None),
        P(None, None, "dp", None, None),
        P(),
        P("section", None, None, None, None),
        P("section", None, None, None, None),
        P("section", None, None, None, None),
        P("section", None, None, None),
        P("section", None, None, None),
        P("section", None, None, None),
        P("section", None, None),
        P("section", None, None),
        P("section", None, None),
        P("section", None, None),
    )
    out_specs = (
        P("section", None, None, "dp", None, None),
        P("section", None, None, "dp", None, None),
        P("section", None, None, None, None),
        P("section", None, None, None, None),
        P("section", None, None, None, None),
        P("section", None, None, None),
        P("section", None, None, None),
        P("section", None, None, None),
        P("section", None, None),
        P("section", None, None),
        P("section", None, None),
        P("section", None, None),
    )
    return jax.shard_map(
        on_device, mesh=mesh, in_specs=in_specs, out_specs=out_specs, check_vma=False
    )
```

profile of v0, /device:TPU:0, one launch (start us, length us, event | category | flops | bytes accessed | tf_op | source)
XLA Modules:
  0.0 2862.1 jit_solution(18001067553535781884)
XLA Ops:
  19.4 43.5 %psum.274 = f32[384]{0:T(512)S(1)} all-reduce(f32[384]{0:T(512)S(1)} %pad_maximum_fusion.98), channel_id=1, replica_groups=mesh['section'=2,'dp'=16] {'dp'}, use_global_device_ids=true, to_apply=%region_4.5 | all-reduce | flops 384 | bytes 3072 | tf_op jit(solution)/shard_map/psum | solution.py:167
  98.4 40.1 %psum.275 = f32[768]{0:T(1024)S(1)} all-reduce(f32[768]{0:T(1024)S(1)} %pad_maximum_fusion.74), channel_id=1, replica_groups=mesh['section'=2,'dp'=16] {'dp'}, use_global_device_ids=true, to_apply=%region_7.8 | all-reduce | flops 768 | bytes 6144 | tf_op jit(solution)/shard_map/psum | solution.py:167
  170.0 42.2 %psum.276 = f32[1024]{0:T(1024)S(1)} all-reduce(f32[1024]{0:T(1024)S(1)} %pad_maximum_fusion.75), channel_id=1, replica_groups=mesh['section'=2,'dp'=16] {'dp'}, use_global_device_ids=true, to_apply=%region_10.11 | all-reduce | flops 1024 | bytes 8192 | tf_op jit(solution)/shard_map/psum | solution.py:167
  218.9 37.0 %psum.279 = f32[384]{0:T(512)S(1)} all-reduce(f32[384]{0:T(512)S(1)} %pad_maximum_fusion.99), channel_id=1, replica_groups=mesh['section'=2,'dp'=16] {'dp'}, use_global_device_ids=true, to_apply=%region_15.16 | all-reduce | flops 384 | bytes 3072 | tf_op jit(solution)/shard_map/psum | solution.py:167
  289.0 41.9 %psum.280 = f32[768]{0:T(1024)S(1)} all-reduce(f32[768]{0:T(1024)S(1)} %pad_maximum_fusion.76), channel_id=1, replica_groups=mesh['section'=2,'dp'=16] {'dp'}, use_global_device_ids=true, to_apply=%region_18.19 | all-reduce | flops 768 | bytes 6144 | tf_op jit(solution)/shard_map/psum | solution.py:167
  364.6 41.8 %psum.281 = f32[1024]{0:T(1024)S(1)} all-reduce(f32[1024]{0:T(1024)S(1)} %pad_maximum_fusion.77), channel_id=1, replica_groups=mesh['section'=2,'dp'=16] {'dp'}, use_global_device_ids=true, to_apply=%region_21.22 | all-reduce | flops 1024 | bytes 8192 | tf_op jit(solution)/shard_map/psum | solution.py:167
  495.9 42.1 %psum.285 = f32[768]{0:T(1024)S(1)} all-reduce(f32[768]{0:T(1024)S(1)} %pad_maximum_fusion.78), channel_id=1, replica_groups=mesh['section'=2,'dp'=16] {'dp'}, use_global_device_ids=true, to_apply=%region_29.30 | all-reduce | flops 768 | bytes 6144 | tf_op jit(solution)/shard_map/psum | solution.py:167
  572.0 42.1 %psum.286 = f32[1024]{0:T(1024)S(1)} all-reduce(f32[1024]{0:T(1024)S(1)} %pad_maximum_fusion.79), channel_id=1, replica_groups=mesh['section'=2,'dp'=16] {'dp'}, use_global_device_ids=true, to_apply=%region_32.33 | all-reduce | flops 1024 | bytes 8192 | tf_op jit(solution)/shard_map/psum | solution.py:167
  621.3 37.0 %psum.289 = f32[384]{0:T(512)S(1)} all-reduce(f32[384]{0:T(512)S(1)} %pad_maximum_fusion.101), channel_id=1, replica_groups=mesh['section'=2,'dp'=16] {'dp'}, use_global_device_ids=true, to_apply=%region_37.38 | all-reduce | flops 384 | bytes 3072 | tf_op jit(solution)/shard_map/psum | solution.py:167
  689.6 42.5 %psum.290 = f32[768]{0:T(1024)S(1)} all-reduce(f32[768]{0:T(1024)S(1)} %pad_maximum_fusion.80), channel_id=1, replica_groups=mesh['section'=2,'dp'=16] {'dp'}, use_global_device_ids=true, to_apply=%region_40.41 | all-reduce | flops 768 | bytes 6144 | tf_op jit(solution)/shard_map/psum | solution.py:167
  765.9 41.8 %psum.291 = f32[1024]{0:T(1024)S(1)} all-reduce(f32[1024]{0:T(1024)S(1)} %pad_maximum_fusion.81), channel_id=1, replica_groups=mesh['section'=2,'dp'=16] {'dp'}, use_global_device_ids=true, to_apply=%region_43.44 | all-reduce | flops 1024 | bytes 8192 | tf_op jit(solution)/shard_map/psum | solution.py:167
  902.8 40.2 %psum.354 = f32[768]{0:T(1024)S(1)} all-reduce(f32[768]{0:T(1024)S(1)} %pad_maximum_fusion.82), channel_id=1, replica_groups=mesh['section'=2,'dp'=16] {'dp'}, use_global_device_ids=true, to_apply=%region_51.52 | all-reduce | flops 768 | bytes 6144 | tf_op jit(solution)/shard_map/psum | solution.py:167
  975.8 42.1 %psum.355 = f32[1024]{0:T(1024)S(1)} all-reduce(f32[1024]{0:T(1024)S(1)} %pad_maximum_fusion.83), channel_id=1, replica_groups=mesh['section'=2,'dp'=16] {'dp'}, use_global_device_ids=true, to_apply=%region_54.55 | all-reduce | flops 1024 | bytes 8192 | tf_op jit(solution)/shard_map/psum | solution.py:167
  1026.8 36.8 %psum.356 = f32[384]{0:T(512)S(1)} all-reduce(f32[384]{0:T(512)S(1)} %pad_maximum_fusion.103), channel_id=1, replica_groups=mesh['section'=2,'dp'=16] {'dp'}, use_global_device_ids=true, to_apply=%region_59.60 | all-reduce | flops 384 | bytes 3072 | tf_op jit(solution)/shard_map/psum | solution.py:167
  1099.6 42.8 %psum.357 = f32[768]{0:T(1024)S(1)} all-reduce(f32[768]{0:T(1024)S(1)} %pad_maximum_fusion.84), channel_id=1, replica_groups=mesh['section'=2,'dp'=16] {'dp'}, use_global_device_ids=true, to_apply=%region_62.63 | all-reduce | flops 768 | bytes 6144 | tf_op jit(solution)/shard_map/psum | solution.py:167
  1180.0 42.1 %psum.358 = f32[1024]{0:T(1024)S(1)} all-reduce(f32[1024]{0:T(1024)S(1)} %pad_maximum_fusion.85), channel_id=1, replica_groups=mesh['section'=2,'dp'=16] {'dp'}, use_global_device_ids=true, to_apply=%region_65.66 | all-reduce | flops 1024 | bytes 8192 | tf_op jit(solution)/shard_map/psum | solution.py:167
  1229.1 36.8 %psum.359 = f32[1024]{0:T(1024)S(1)} all-reduce(f32[1024]{0:T(1024)S(1)} %pad_maximum_fusion.86), channel_id=1, replica_groups=mesh['section'=2,'dp'=16] {'dp'}, use_global_device_ids=true, to_apply=%region_70.71 | all-reduce | flops 1024 | bytes 8192 | tf_op jit(solution)/shard_map/psum | solution.py:176
  1319.8 40.5 %psum.360 = f32[768]{0:T(1024)S(1)} all-reduce(f32[768]{0:T(1024)S(1)} %pad_maximum_fusion.87), channel_id=1, replica_groups=mesh['section'=2,'dp'=16] {'dp'}, use_global_device_ids=true, to_apply=%region_73.74 | all-reduce | flops 768 | bytes 6144 | tf_op jit(solution)/shard_map/psum | solution.py:176
  1395.1 40.6 %psum.361 = f32[384]{0:T(512)S(1)} all-reduce(f32[384]{0:T(512)S(1)} %pad_maximum_fusion.104), channel_id=1, replica_groups=mesh['section'=2,'dp'=16] {'dp'}, use_global_device_ids=true, to_apply=%region_76.77 | all-reduce | flops 384 | bytes 3072 | tf_op jit(solution)/shard_map/psum | solution.py:176
  1530.0 40.0 %psum.363 = f32[768]{0:T(1024)S(1)} all-reduce(f32[768]{0:T(1024)S(1)} %pad_maximum_fusion.89), channel_id=1, replica_groups=mesh['section'=2,'dp'=16] {'dp'}, use_global_device_ids=true, to_apply=%region_84.85 | all-reduce | flops 768 | bytes 6144 | tf_op jit(solution)/shard_map/psum | solution.py:176
  1610.7 42.1 %psum.364 = f32[384]{0:T(512)S(1)} all-reduce(f32[384]{0:T(512)S(1)} %pad_maximum_fusion.105), channel_id=1, replica_groups=mesh['section'=2,'dp'=16] {'dp'}, use_global_device_ids=true, to_apply=%region_87.88 | all-reduce | flops 384 | bytes 3072 | tf_op jit(solution)/shard_map/psum | solution.py:176
  1763.1 40.1 %psum.366 = f32[768]{0:T(1024)S(1)} all-reduce(f32[768]{0:T(1024)S(1)} %pad_maximum_fusion.91), channel_id=1, replica_groups=mesh['section'=2,'dp'=16] {'dp'}, use_global_device_ids=true, to_apply=%region_95.96 | all-reduce | flops 768 | bytes 6144 | tf_op jit(solution)/shard_map/psum | solution.py:176
  1836.9 41.1 %psum.367 = f32[384]{0:T(512)S(1)} all-reduce(f32[384]{0:T(512)S(1)} %pad_maximum_fusion.106), channel_id=1, replica_groups=mesh['section'=2,'dp'=16] {'dp'}, use_global_device_ids=true, to_apply=%region_98.99 | all-reduce | flops 384 | bytes 3072 | tf_op jit(solution)/shard_map/psum | solution.py:176
  1885.8 37.0 %psum.368 = f32[1024]{0:T(1024)S(1)} all-reduce(f32[1024]{0:T(1024)S(1)} %pad_maximum_fusion.92), channel_id=1, replica_groups=mesh['section'=2,'dp'=16] {'dp'}, use_global_device_ids=true, to_apply=%region_103.104 | all-reduce | flops 1024 | bytes 8192 | tf_op jit(solution)/shard_map/psum | solution.py:176
  1969.0 40.4 %psum.369 = f32[768]{0:T(1024)S(1)} all-reduce(f32[768]{0:T(1024)S(1)} %pad_maximum_fusion.93), channel_id=1, replica_groups=mesh['section'=2,'dp'=16] {'dp'}, use_global_device_ids=true, to_apply=%region_106.107 | all-reduce | flops 768 | bytes 6144 | tf_op jit(solution)/shard_map/psum | solution.py:176
  2053.1 42.1 %psum.370 = f32[384]{0:T(512)S(1)} all-reduce(f32[384]{0:T(512)S(1)} %pad_maximum_fusion.107), channel_id=1, replica_groups=mesh['section'=2,'dp'=16] {'dp'}, use_global_device_ids=true, to_apply=%region_109.110 | all-reduce | flops 384 | bytes 3072 | tf_op jit(solution)/shard_map/psum | solution.py:176
  2207.3 40.2 %psum.372 = f32[768]{0:T(1024)S(1)} all-reduce(f32[768]{0:T(1024)S(1)} %pad_maximum_fusion.95), channel_id=1, replica_groups=mesh['section'=2,'dp'=16] {'dp'}, use_global_device_ids=true, to_apply=%region_117.118 | all-reduce | flops 768 | bytes 6144 | tf_op jit(solution)/shard_map/psum | solution.py:176
  2279.7 42.0 %psum.373 = f32[384]{0:T(512)S(1)} all-reduce(f32[384]{0:T(512)S(1)} %pad_maximum_fusion.108), channel_id=1, replica_groups=mesh['section'=2,'dp'=16] {'dp'}, use_global_device_ids=true, to_apply=%region_120.121 | all-reduce | flops 384 | bytes 3072 | tf_op jit(solution)/shard_map/psum | solution.py:176
  2329.4 36.7 %psum.374 = f32[1024]{0:T(1024)S(1)} all-reduce(f32[1024]{0:T(1024)S(1)} %pad_maximum_fusion.96), channel_id=1, replica_groups=mesh['section'=2,'dp'=16] {'dp'}, use_global_device_ids=true, to_apply=%region_125.126 | all-reduce | flops 1024 | bytes 8192 | tf_op jit(solution)/shard_map/psum | solution.py:176
  2406.3 42.8 %psum.375 = f32[768]{0:T(1024)S(1)} all-reduce(f32[768]{0:T(1024)S(1)} %pad_maximum_fusion.97), channel_id=1, replica_groups=mesh['section'=2,'dp'=16] {'dp'}, use_global_device_ids=true, to_apply=%region_128.129 | all-reduce | flops 768 | bytes 6144 | tf_op jit(solution)/shard_map/psum | solution.py:176
  2482.0 41.9 %psum.376 = f32[384]{0:T(512)S(1)} all-reduce(f32[384]{0:T(512)S(1)} %pad_maximum_fusion.109), channel_id=1, replica_groups=mesh['section'=2,'dp'=16] {'dp'}, use_global_device_ids=true, to_apply=%region_131.132 | all-reduce | flops 384 | bytes 3072 | tf_op jit(solution)/shard_map/psum | solution.py:176
  2580.0 263.0 %all-reduce.15.cloned.1.call-done = (f32[2,9,512,128]{3,2,1,0:T(8,128)}, f32[1,2,9,128,384]{4,3,2,1,0:T(8,128)}, f32[1,2,384,192]{2,3,1,0:T(8,128)}, f32[1,2,384,384]{3,2,1,0:T(8,128)}, f32[1,2,192,384]{3,2,1,0:T(8,128)}) async-done(((f32[2,9,512,128]{3,2,1,0:T(8,128)}, f32[1,2,9,128,384]{4,3,2,1,0:T(8,128)}, f32[1,2,384,192]{2,3,1,0:T(8,128)}, f32[1,2,384,384]{3,2,1,0:T(8,128)}, ...) | async-done | bytes 10616848 | tf_op jit(solution)/shard_map/psum | solution.py:506
  (2178 shorter events, 1288.6 us)
Async XLA Ops:
  70.2 20.6 all-to-all-start
  146.8 18.8 all-to-all-start.1
  342.1 18.0 all-to-all-start.3
  470.4 17.1 all-to-all-start.4
  549.3 18.2 all-to-all-start.5
  743.4 18.0 all-to-all-start.7
  873.7 21.8 all-to-all-start.8
  951.3 20.0 all-to-all-start.9
  1070.1 21.4 all-to-all-start.10
  1151.9 23.6 all-to-all-start.11
  1280.7 30.9 %all-to-all-start.12 = ((bf16[1,8,80,384]{3,1,0,2:T(8,128)(2,1)}), bf16[1,8,80,384]{3,1,0,2:T(8,128)(2,1)}, u32[]{:S(2)}, u32[]{:S(2)}) async-start(bf16[1,8,80,384]{3,1,0,2:T(8,128)(2,1)} %copy.1314), calls=%async_computation.12 | async-start | bytes 983040 | tf_op jit(solution)/shard_map/all_to_all | solution.py:309
  1285.0 20.6 collective-permute-start.15
  1286.3 19.3 collective-permute-start.14
  1372.3 17.8 all-to-all-start.13
  1495.7 25.9 all-to-all-start.14
  1500.0 20.2 collective-permute-start.17
  1501.3 18.9 collective-permute-start.16
  1582.3 23.9 all-to-all-start.15
  1725.2 29.6 %all-to-all-start.16 = ((bf16[1,8,80,384]{3,1,0,2:T(8,128)(2,1)}), bf16[1,8,80,384]{3,1,0,2:T(8,128)(2,1)}, u32[]{:S(2)}, u32[]{:S(2)}) async-start(bf16[1,8,80,384]{3,1,0,2:T(8,128)(2,1)} %copy.1370), calls=%async_computation.16 | async-start | bytes 983040 | tf_op jit(solution)/shard_map/all_to_all | solution.py:309
  1729.5 20.4 collective-permute-start.20
  1730.8 19.0 collective-permute-start.19
  1816.4 17.3 all-to-all-start.17
  1936.1 24.7 all-to-all-start.18
  1940.3 19.0 collective-permute-start.22
  1941.6 17.7 collective-permute-start.21
  2023.5 24.5 all-to-all-start.19
  2167.5 31.6 %all-to-all-start.20 = ((bf16[1,8,80,384]{3,1,0,2:T(8,128)(2,1)}), bf16[1,8,80,384]{3,1,0,2:T(8,128)(2,1)}, u32[]{:S(2)}, u32[]{:S(2)}) async-start(bf16[1,8,80,384]{3,1,0,2:T(8,128)(2,1)} %copy.1426), calls=%async_computation.20 | async-start | bytes 983040 | tf_op jit(solution)/shard_map/all_to_all | solution.py:309
  2171.7 20.1 collective-permute-start.25
  2173.0 18.8 collective-permute-start.24
  2376.1 22.0 all-to-all-start.22
  2464.8 378.1 %all-reduce.15.cloned.1.call-start = ((), (), s32[]{:S(2)}) async-start(), calls=%async_computation.24 | async-start | bytes 21233664 | tf_op jit(solution)/shard_map/psum | solution.py:506
  2537.6 18.2 collective-permute-start.27
  (566 other events, 10716.9 us)
Sparse Core Ops, SparseCore 0:
  2528.8 314.1 all-reduce.14
where the time goes:
time: 2880 us; the launch traced here: 2860 us
  blocking collectives  1440 us (50%)
  matrix products  431 us (15%)
  waiting for transfers between devices  276 us (10%)
  local copies, waits for them, and re-layouts  266 us (9%)
  other arithmetic  211 us (7%)
  starting transfers between devices  185 us (6%)
  between operations  49.8 us (2%)
    psum x18, blocking collectives, moments(): totals = lax.psum(jnp.concatenate(pieces), 'dp')  729 us
    psum x18, blocking collectives, grad_moments(): totals = lax.psum(jnp.concatenate(pieces), 'dp')  714 us
    psum x1, waiting for transfers between devices, on_device(): lax.psum((kernel_acc[0], kernel_acc[1], kernel_acc[2], kernel_acc[3], ker...  263 us
    dot_general x108, matrix products, kernel_grad(): jnp.einsum('mrwi,mrwo->io', window, grad_out, preferred_element_type=jnp....  87.1 us
    dot_general x48, matrix products, height_adjoint(): return jnp.einsum('kn,mkfc->mnfc', table, entry, precision=PRECISE)  81.7 us
    conv_general_dilated x120, local copies, waits for them, and re-layouts, conv_rows(): lax.conv_general_dilated(padded, shaped, (1, 1), 'VALID', dimension_numbe...  79.4 us
    unnamed x1108, local copies, waits for them, and re-layouts  70.5 us
    dot_general x48, matrix products, height_apply(): return jnp.einsum('kn,mnfc->mkfc', table, entry, precision=PRECISE)  64.5 us
  transfers between devices with their start and end apart: 53, of which 12 were waited for; matrix products, arithmetic and copies ran while one was open for 12% of the time, Pallas kernels for 0%

commit v1 on v0

--- a/solution.py
+++ b/solution.py
@@ -1,6 +1,8 @@
 import jax
 import jax.numpy as jnp
 from jax import lax
+from jax.experimental import pallas as pl
+from jax.experimental.pallas import tpu as pltpu
 from jax.sharding import PartitionSpec as P
 
 CL = 128
@@ -524,6 +526,1019 @@
     )
 
 
+F32 = jnp.float32
+BF16 = jnp.bfloat16
+MESH = pl.DeviceIdType.MESH
+MEMBERS = 16
+ROWS = 8
+LAYERS = 4
+PAIRS = 4
+HALF = 192
+FULL = 384
+SLOTS = 640
+GRAD_ROWS = 10752
+AT_KL = 0
+AT_KG = 4608
+AT_E = 8064
+AT_M = 8704
+AT_R = 9856
+SECTION_NAMES = ("one", "two", "out")
+
+
+def dot(a, b):
+    return lax.dot_general(a, b, (((1,), (0,)), ((), ())), preferred_element_type=F32)
+
+
+def dot_nt(a, b):
+    return lax.dot_general(a, b, (((1,), (1,)), ((), ())), preferred_element_type=F32)
+
+
+def dot_tn(a, b):
+    return lax.dot_general(a, b, (((0,), (0,)), ((), ())), preferred_element_type=F32)
+
+
+def sigmoid(v):
+    return 0.5 * jnp.tanh(0.5 * v) + 0.5
+
+
+def fold(v):
+    return jnp.sum(v.reshape(v.shape[0] // 8, 8, v.shape[1]), axis=0)
+
+
+def wide(row, lanes):
+    whole, rest = divmod(lanes, 128)
+    parts = [row] * whole + ([row[:, :rest]] if rest else [])
+    return jnp.concatenate(parts, axis=1)
+
+
+def network_kernel(
+    inputs, cot, shapes, ll, gl, lg, red, mix, exp, par, run, tables, counts,
+    out_y, out_g, out_w, out_p,
+    w_c, w_gl, w_r, w_m, w_e, pars, acts, shifted, halo, v1, u, spec, mixed, tsum, v34,
+    pmask, qmask, tf, tft, tg, tgt, hf, hi, vab, e2, dq, ds, g, gblk, at, gw,
+    ssum, rsum, send, recv, stats, stats_far,
+    sem_w, sem_in, sem_cot, sem_halo_s, sem_halo_r, sem_ar_s, sem_ar_r, sem_aa_s, sem_aa_r,
+    sem_y_s, sem_y_r, sem_g_s, sem_g_r, sem_gw, sem_st,
+):
+    s = lax.axis_index("section")
+    d = lax.axis_index("dp")
+    n_dp = lax.axis_size("dp")
+    per = n_dp // 2
+    grp = lax.div(d, per)
+    me = 2 * lax.rem(d, per) + s
+    first = (me == 0).astype(F32)
+
+    def member(group, k):
+        return (lax.rem(k, 2), group * per + lax.div(k, 2))
+
+    barrier = pltpu.get_barrier_semaphore()
+    total = 2 * n_dp
+    flat = s * n_dp + d
+
+    def greet(i, c):
+        other = lax.rem(flat + 1 + i, total)
+        pl.semaphore_signal(
+            barrier, inc=1, device_id=(lax.div(other, n_dp), lax.rem(other, n_dp)), device_id_type=MESH
+        )
+        return c
+
+    lax.fori_loop(0, total - 1, greet, 0)
+
+    own = pl.ds(2 * s, 2)
+    places = [
+        (red, w_r.at[own]),
+        (par, pars.at[own]),
+        (ll, w_c.at[own, :, :, 0:CL]),
+        (lg, w_c.at[own, :, :, CL:]),
+        (gl, w_gl.at[own]),
+        (mix, w_m.at[own]),
+        (exp, w_e.at[own]),
+    ]
+    local_w = [pltpu.make_async_copy(a, b, sem_w.at[0, i]) for i, (a, b) in enumerate(places)]
+    for c in local_w:
+        c.start()
+
+    pl.semaphore_wait(barrier, total - 1)
+
+    goal = (lax.rem(d, 2), s * per + lax.div(d, 2))
+    stays = (goal[0] == s) & (goal[1] == d)
+
+    def push_in(source, target, sems):
+        @pl.when(stays)
+        def _():
+            pltpu.make_async_copy(source, target, sems.at[0]).start()
+
+        @pl.when(jnp.logical_not(stays))
+        def _():
+            pltpu.make_async_remote_copy(
+                source, target, sems.at[0], sems.at[1], device_id=goal, device_id_type=MESH
+            ).start()
+
+    def wait_in(source, target, sems):
+        @pl.when(stays)
+        def _():
+            pltpu.make_async_copy(source, target, sems.at[0]).wait()
+
+        @pl.when(jnp.logical_not(stays))
+        def _():
+            pltpu.make_async_remote_copy(
+                source, target, sems.at[0], sems.at[1], device_id=goal, device_id_type=MESH
+            ).wait()
+
+    push_in(inputs.at[s], acts.at[0], sem_in)
+    partner = (1 - s, d)
+    remote_w = [
+        pltpu.make_async_remote_copy(
+            a, b, sem_w.at[1, i], sem_w.at[2, i], device_id=partner, device_id_type=MESH
+        )
+        for i, (a, b) in enumerate(places)
+    ]
+    for c in remote_w:
+        c.start()
+
+    height = shapes[grp, 0]
+    width = shapes[grp, 1]
+    col = lax.broadcasted_iota(jnp.int32, (128, 128), 0)
+    for q in range(PAIRS):
+        for h in range(2):
+            row_ok = (ROWS * me + 2 * q + h < height).astype(F32)
+            pmask[q, h * 128 : (h + 1) * 128, :] = (col < width).astype(F32) * row_ok
+    for f in range(4):
+        f_ok = (4 * me + f <= lax.div(width, 2)).astype(F32)
+        qmask[f * 128 : (f + 1) * 128, :] = (col < height).astype(F32) * f_ok
+    qmask[512:640, :] = (col < height).astype(F32) * (64 <= lax.div(width, 2)).astype(F32) * first
+    inv_n = counts[0:1, :]
+    inv_ns = counts[1:2, :]
+
+    row_a = lax.broadcasted_iota(jnp.int32, (128, 512), 0)
+    col_a = lax.broadcasted_iota(jnp.int32, (128, 512), 1)
+    r_of = (col_a >> 5) * 8 + ((col_a & 31) >> 3) * 2 + (col_a & 1)
+    sel_r = (row_a == r_of).astype(F32).astype(BF16)
+    f_of = (col_a >> 1) & 3
+    row_b = lax.broadcasted_iota(jnp.int32, (512, 128), 0)
+    col_b = lax.broadcasted_iota(jnp.int32, (512, 128), 1)
+    r_ob = (row_b >> 5) * 8 + ((row_b & 31) >> 3) * 2 + (row_b & 1)
+    sel_rt = (col_b == r_ob).astype(F32).astype(BF16)
+    f_ob = (row_b >> 1) & 3
+    for part in range(2):
+        base = tables[part].astype(BF16)
+        spread = dot(base, sel_r)
+        spread_t = dot(sel_rt, base)
+        for f in range(4):
+            hf[f, part * 128 : (part + 1) * 128, :] = jnp.where(f_of == f, spread, 0.0).astype(BF16)
+            at_col = part * 512 + f * 128
+            hi[:, at_col : at_col + 128] = jnp.where(f_ob == f, spread_t, 0.0).astype(BF16)
+    row_c = lax.broadcasted_iota(jnp.int32, (128, 128), 0)
+    sel_f = ((row_c >> 1) == lax.broadcasted_iota(jnp.int32, (128, 128), 1)).astype(F32).astype(BF16)
+    for which, (plain, flipped_table) in enumerate(((tf, tft), (tg, tgt))):
+        for part in range(2):
+            spread = dot(sel_f, tables[2 + 2 * which + part].astype(BF16))
+            spread_t = jnp.transpose(spread)
+            for h in range(2):
+                rows = slice(part * 128, (part + 1) * 128)
+                cols = slice(h * 128, (h + 1) * 128)
+                plain[rows, cols] = jnp.where((row_c & 1) == h, spread, 0.0).astype(BF16)
+                flipped_table[cols, rows] = jnp.where(
+                    (lax.broadcasted_iota(jnp.int32, (128, 128), 1) & 1) == h, spread_t, 0.0
+                ).astype(BF16)
+    stats[...] = jnp.zeros_like(stats)
+    ssum[...] = jnp.zeros_like(ssum)
+    shifted[0] = jnp.zeros((128, 1536), BF16)
+    shifted[9] = jnp.zeros((128, 1536), BF16)
+    gw[AT_M - 64 : AT_M, :] = jnp.zeros((64, 128), BF16)
+    gw[GRAD_ROWS - 128 :, :] = jnp.zeros((128, 128), BF16)
+
+    def sums_start(slot):
+        rsum[slot, me] = ssum[slot]
+
+        def go(i, c):
+            k = lax.rem(me + 1 + i, MEMBERS)
+            pltpu.make_async_remote_copy(
+                ssum.at[slot], rsum.at[slot, me], sem_ar_s.at[slot, k], sem_ar_r.at[slot, me],
+                device_id=member(grp, k), device_id_type=MESH,
+            ).start()
+            return c
+
+        lax.fori_loop(0, MEMBERS - 1, go, 0)
+
+    def sums_wait(slot, lanes):
+        def go(i, c):
+            k = lax.rem(me + 1 + i, MEMBERS)
+            pltpu.make_async_remote_copy(
+                ssum.at[slot], rsum.at[slot, k], sem_ar_s.at[slot, k], sem_ar_r.at[slot, k],
+                device_id=member(grp, k), device_id_type=MESH,
+            ).wait()
+            return c
+
+        lax.fori_loop(0, MEMBERS - 1, go, 0)
+        tot = jnp.sum(rsum[slot], axis=0)
+        tiles = (lanes + 127) // 128
+        one = jnp.concatenate([tot[i : i + 1] for i in range(tiles)], axis=1)[:, :lanes]
+        two = jnp.concatenate([tot[4 + i : 5 + i] for i in range(tiles)], axis=1)[:, :lanes]
+        return one, two
+
+    def put_sums(slot, one, two):
+        lanes = one.shape[1]
+        for base_row, part in ((0, one), (4, two)):
+            flat_part = jnp.sum(part, axis=0, keepdims=True)
+            for i in range((lanes + 127) // 128):
+                w = min(128, lanes - i * 128)
+                ssum[slot, base_row + i : base_row + i + 1, 0:w] = flat_part[:, i * 128 : i * 128 + w]
+
+    def swap_start(slot):
+        recv[slot, me] = send[slot, me]
+
+        def go(i, c):
+            k = lax.rem(me + 1 + i, MEMBERS)
+            pltpu.make_async_remote_copy(
+                send.at[slot, k], recv.at[slot, me], sem_aa_s.at[slot, k], sem_aa_r.at[slot, me],
+                device_id=member(grp, k), device_id_type=MESH,
+            ).start()
+            return c
+
+        lax.fori_loop(0, MEMBERS - 1, go, 0)
+
+    def swap_wait(slot):
+        def go(i, c):
+            k = lax.rem(me + 1 + i, MEMBERS)
+            pltpu.make_async_remote_copy(
+                send.at[slot, k], recv.at[slot, k], sem_aa_s.at[slot, k], sem_aa_r.at[slot, k],
+                device_id=member(grp, k), device_id_type=MESH,
+            ).wait()
+            return c
+
+        lax.fori_loop(0, MEMBERS - 1, go, 0)
+
+    def halo_copies():
+        up = pltpu.make_async_remote_copy(
+            shifted.at[1, :, 512:1024], halo.at[1], sem_halo_s.at[0], sem_halo_r.at[1],
+            device_id=member(grp, lax.rem(me + MEMBERS - 1, MEMBERS)), device_id_type=MESH,
+        )
+        down = pltpu.make_async_remote_copy(
+            shifted.at[8, :, 512:1024], halo.at[0], sem_halo_s.at[1], sem_halo_r.at[0],
+            device_id=member(grp, lax.rem(me + 1, MEMBERS)), device_id_type=MESH,
+        )
+        return up, down
+
+    has_up = me > 0
+    has_down = me < MEMBERS - 1
+
+    def halo_start():
+        up, down = halo_copies()
+
+        @pl.when(has_up)
+        def _():
+            up.start()
+
+        @pl.when(has_down)
+        def _():
+            down.start()
+
+    def put_shifted(index, x, flip):
+        at_col = lax.broadcasted_iota(jnp.int32, (128, 512), 0)
+        before = jnp.where(at_col == 0, 0.0, pltpu.roll(x, 1, 0))
+        after = jnp.where(at_col == 127, 0.0, pltpu.roll(x, 127, 0))
+        parts = (after, x, before) if flip else (before, x, after)
+        for j, part in enumerate(parts):
+            shifted[index, :, j * 512 : (j + 1) * 512] = part.astype(BF16)
+
+    def halo_wait(flip):
+        up, down = halo_copies()
+
+        @pl.when(has_up)
+        def _():
+            up.wait_send()
+            down.wait_recv()
+            put_shifted(0, halo[0].astype(F32), flip)
+
+        @pl.when(has_down)
+        def _():
+            down.wait_send()
+            up.wait_recv()
+            put_shifted(9, halo[1].astype(F32), flip)
+
+    lane = lax.broadcasted_iota(jnp.int32, (128, FULL), 1)
+    low = lane < HALF
+
+    def width_out(slot, h, table, get):
+        parts = []
+        for q in (2 * h, 2 * h + 1):
+            x = dot(table[...], get(q))
+            both = jnp.concatenate([x[:128], x[128:]], axis=1)
+            parts.append(both.reshape(MEMBERS, 8, FULL))
+        send[slot, :, pl.ds(pl.multiple_of(16 * h, 16), 16), :] = jnp.concatenate(parts, axis=1).astype(BF16)
+
+    def width_back(slot, h, table):
+        block = recv[slot, :, pl.ds(pl.multiple_of(16 * h, 16), 16), :].astype(F32)
+        results = []
+        for o in range(2):
+            z = block[:, 8 * o : 8 * o + 8, :].reshape(128, FULL)
+            zi = pltpu.roll(z, HALF, 1)
+            stacked = jnp.concatenate([z[:, :HALF], zi[:, :HALF]], axis=0).astype(BF16)
+            results.append(dot(table[...], stacked))
+        return results
+
+    def rows_forward_into(slot, put):
+        x = recv[slot].reshape(512, FULL)
+        for f in range(4):
+            both = dot(hf[f], x)
+            a, b = both[:128], both[128:]
+            turned = pltpu.roll(b, HALF, 1)
+            if f == 0:
+                rest = 1.0 - first
+                put(0, jnp.where(low, a + rest * turned, rest * a - turned))
+                put(4, jnp.where(low, pltpu.roll(a, HALF, 1), -b) * first)
+            else:
+                put(f, jnp.where(low, a + turned, a - turned))
+
+    def rows_inverse_from(slot, get):
+        last = get(4)
+        for f in range(4):
+            v = get(f)
+            turned = pltpu.roll(v, HALF, 1)
+            if f == 0:
+                rest = 1.0 - first
+                a = jnp.where(low, v, rest * v + first * pltpu.roll(last, HALF, 1))
+                b = jnp.where(low, -turned, rest * turned - first * last)
+            else:
+                a = v
+                b = jnp.where(low, -turned, turned)
+            vab[f * 128 : (f + 1) * 128, :] = a.astype(BF16)
+            vab[512 + f * 128 : 640 + f * 128, :] = b.astype(BF16)
+
+        def go(c, carry):
+            z = dot(hi[pl.ds(pl.multiple_of(c * 256, 256), 256), :], vab[...])
+            send[slot, pl.ds(c * 8, 8)] = z.astype(BF16).reshape(8, 32, FULL)
+            return carry
+
+        lax.fori_loop(0, 2, go, 0)
+
+    def moments(layer, which, lanes, one, two, inv_count):
+        count = wide(inv_count, lanes)
+        mean = one * count
+        var = two * count - mean * mean
+        inv = lax.rsqrt(var + EPSILON)
+        stats[layer, which : which + 1, 0:lanes] = mean
+        stats[layer, 3 + which : 4 + which, 0:lanes] = inv
+        stats[layer, 6 + which : 7 + which, 0:lanes] = var
+        scale = pars[layer, which : which + 1, 0:lanes] * inv
+        shift = pars[layer, 3 + which : 4 + which, 0:lanes] - mean * scale
+        return scale, shift
+
+    def affine(layer, which, lanes):
+        mean = stats[layer, which : which + 1, 0:lanes]
+        inv = stats[layer, 3 + which : 4 + which, 0:lanes]
+        gain = pars[layer, which : which + 1, 0:lanes]
+        return mean, inv, gain, pars[layer, 3 + which : 4 + which, 0:lanes]
+
+    def keep_grad_sums(layer, which, lanes, one, two):
+        stats[layer, 9 + which : 10 + which, 0:lanes] = one
+        stats[layer, 12 + which : 13 + which, 0:lanes] = two
+
+    zero_of = lambda lanes: jnp.zeros((8, lanes), F32)
+
+    def conv_pair(layer, c):
+        loc = jnp.zeros((256, 512), F32)
+        glo = jnp.zeros((256, 128), F32)
+        for i in range(3):
+            a_loc = jnp.concatenate(
+                [shifted[pl.ds(2 * c + i, 2), :, j * 512 : j * 512 + 128].reshape(256, 128) for j in range(3)], axis=1
+            )
+            a_glo = jnp.concatenate(
+                [shifted[pl.ds(2 * c + i, 2), :, j * 512 + 128 : (j + 1) * 512].reshape(256, 384) for j in range(3)],
+                axis=1,
+            )
+            loc = loc + dot(a_loc, w_c[layer, 3 * i : 3 * i + 3].reshape(384, 512))
+            glo = glo + dot(a_glo, w_gl[layer, 3 * i : 3 * i + 3].reshape(1152, 128))
+        v34[layer, c, :, 0:CL] = loc[:, :CL] + glo
+        v34[layer, c, :, CL:] = loc[:, CL:]
+
+    wait_in(inputs.at[s], acts.at[0], sem_in)
+    push_in(cot.at[s], gblk.at[1], sem_cot)
+
+    def start_row(r, c):
+        q = lax.div(r, 2)
+        pm = pmask[q, pl.ds(pl.multiple_of(lax.rem(r, 2) * 128, 128), 128), :]
+        x = acts[0, r].astype(F32) * wide(pm, 512)
+        acts[0, r] = x.astype(BF16)
+        put_shifted(1 + r, x, False)
+        return c
+
+    lax.fori_loop(0, ROWS, start_row, 0)
+    for c in local_w:
+        c.wait()
+    for c in remote_w:
+        c.wait()
+
+    def y_copy(block):
+        source = acts.at[2 * block + 2]
+        target = out_y.at[grp]
+        goal_now = (block, me)
+        far = pltpu.make_async_remote_copy(
+            source, target, sem_y_s.at[block], sem_y_r.at[grp], device_id=goal_now, device_id_type=MESH
+        )
+        near = pltpu.make_async_copy(source, target, sem_y_s.at[block])
+        return (block == s) & (me == d), far, near
+
+    def g_copy(block):
+        source = gblk.at[2 * block]
+        target = out_g.at[grp]
+        far = pltpu.make_async_remote_copy(
+            source, target, sem_g_s.at[block], sem_g_r.at[grp], device_id=(block, me), device_id_type=MESH
+        )
+        near = pltpu.make_async_copy(source, target, sem_g_s.at[block])
+        return (block == s) & (me == d), far, near
+
+    def start_out(made):
+        here, far, near = made
+
+        @pl.when(here)
+        def _():
+            near.start()
+
+        @pl.when(jnp.logical_not(here))
+        def _():
+            far.start()
+
+    def wait_out(made):
+        here, far, near = made
+
+        @pl.when(here)
+        def _():
+            near.wait()
+
+        @pl.when(jnp.logical_not(here))
+        def _():
+            far.wait_send()
+
+    def forward(layer, carry):
+        halo_start()
+
+        def reduce_pair(q, sums):
+            a = acts[layer, pl.ds(2 * q, 2), :, CL:].reshape(256, CG)
+            v = dot(a, w_r[layer])
+            v1[layer, q] = v
+            return sums[0] + fold(v), sums[1] + fold(v * v)
+
+        put_sums(0, *lax.fori_loop(0, PAIRS, reduce_pair, (zero_of(HALF), zero_of(HALF))))
+        sums_start(0)
+
+        def conv_go(c, carry):
+            conv_pair(layer, c)
+            return carry
+
+        lax.fori_loop(1, 3, conv_go, 0)
+        scale, shift = moments(layer, 0, HALF, *sums_wait(0, HALF), inv_n)
+
+        def spectral_in(h, carry):
+            def get(q):
+                pre = v1[layer, q] * scale + shift
+                x = pre * sigmoid(pre) * wide(pmask[q], HALF)
+                u[q] = x
+                return x.astype(BF16)
+
+            width_out(0, h, tf, get)
+            return carry
+
+        lax.fori_loop(0, 2, spectral_in, 0)
+        swap_start(0)
+        halo_wait(False)
+        lax.fori_loop(0, 2, lambda c, k: conv_go(3 * c, k), 0)
+        swap_wait(0)
+
+        def put(f, y):
+            spec[layer, f * 128 : (f + 1) * 128, :] = y.astype(BF16)
+
+        rows_forward_into(0, put)
+
+        def mix_block(f, sums):
+            at_row = pl.ds(pl.multiple_of(f * 128, 128), 128)
+            v = dot(spec[layer, at_row, :], w_m[layer])
+            mixed[layer, at_row, :] = v
+            return sums[0] + fold(v), sums[1] + fold(v * v)
+
+        put_sums(1, *lax.fori_loop(0, 5, mix_block, (zero_of(FULL), zero_of(FULL))))
+        sums_start(1)
+        scale2, shift2 = moments(layer, 1, FULL, *sums_wait(1, FULL), inv_ns)
+
+        def get_v(f):
+            rows = slice(f * 128, (f + 1) * 128)
+            pre = mixed[layer, rows, :] * scale2 + shift2
+            return pre * sigmoid(pre) * wide(qmask[rows, :], FULL)
+
+        rows_inverse_from(1, get_v)
+        swap_start(1)
+        swap_wait(1)
+
+        def spectral_out(h, sums):
+            backs = width_back(1, h, tgt)
+            one, two = sums
+            for o in range(2):
+                q = 2 * h + o
+                t = (u[q] + backs[o]).astype(BF16)
+                tsum[layer, q] = t
+                pm = pmask[q]
+                v_loc = v34[layer, q, :, 0:CL] * pm
+                v_glo = (v34[layer, q, :, CL:] + dot(t, w_e[layer])) * wide(pm, CG)
+                v34[layer, q, :, 0:CL] = v_loc
+                v34[layer, q, :, CL:] = v_glo
+                v = jnp.concatenate([v_loc, v_glo], axis=1)
+                one = one + fold(v)
+                two = two + fold(v * v)
+            return one, two
+
+        put_sums(2, *lax.fori_loop(0, 2, spectral_out, (zero_of(512), zero_of(512))))
+        sums_start(2)
+        scale3, shift3 = moments(layer, 2, 512, *sums_wait(2, 512), inv_n)
+        odd = lax.rem(layer, 2)
+        oddf = odd.astype(F32)
+
+        def next_row(r, carry):
+            q = lax.div(r, 2)
+            here = pl.ds(pl.multiple_of(lax.rem(r, 2) * 128, 128), 128)
+            pre = v34[layer, q, here, :] * scale3 + shift3
+            x = pre * sigmoid(pre) * wide(pmask[q, here, :], 512)
+            x = x + oddf * acts[layer - odd, r].astype(F32)
+            acts[layer + 1, r] = x.astype(BF16)
+
+            @pl.when(layer < LAYERS - 1)
+            def _():
+                put_shifted(1 + r, x, False)
+
+            return carry
+
+        lax.fori_loop(0, ROWS, next_row, 0)
+
+        @pl.when(odd == 1)
+        def _():
+            start_out(y_copy(lax.div(layer, 2)))
+
+        return carry
+
+    lax.fori_loop(0, LAYERS, forward, 0)
+
+    wait_in(cot.at[s], gblk.at[1], sem_cot)
+
+    def cot_row(r, c):
+        q = lax.div(r, 2)
+        here = pl.ds(pl.multiple_of(lax.rem(r, 2) * 128, 128), 128)
+        x = gblk[1, r].astype(F32) * wide(pmask[q, here, :], 512)
+        gblk[1, r] = x.astype(BF16)
+        g[q, here, :] = x
+        return c
+
+    lax.fori_loop(0, ROWS, cot_row, 0)
+
+    def gw_copy(layer):
+        return pltpu.make_async_copy(gw, out_w.at[layer], sem_gw)
+
+    def backward(step, carry):
+        layer = LAYERS - 1 - step
+        mean3, inv3, gain3, bias3 = affine(layer, 2, 512)
+        scale3 = gain3 * inv3
+        shift3 = bias3 - mean3 * scale3
+
+        def slope_row(r, sums):
+            q = lax.div(r, 2)
+            here = pl.ds(pl.multiple_of(lax.rem(r, 2) * 128, 128), 128)
+            v = v34[layer, q, here, :]
+            pre = v * scale3 + shift3
+            sg = sigmoid(pre)
+            e = g[q, here, :] * wide(pmask[q, here, :], 512) * (sg * (1.0 + pre * (1.0 - sg)))
+            g[q, here, :] = e
+            return sums[0] + fold(e), sums[1] + fold(e * ((v - mean3) * inv3))
+
+        put_sums(3, *lax.fori_loop(0, ROWS, slope_row, (zero_of(512), zero_of(512))))
+        sums_start(3)
+
+        def turn_row(r, carry):
+            at[:, pl.ds(pl.multiple_of(r * 128, 128), 128)] = jnp.transpose(acts[layer, r])
+            return carry
+
+        lax.fori_loop(0, ROWS, turn_row, 0)
+        one3, two3 = sums_wait(3, 512)
+        keep_grad_sums(layer, 2, 512, one3, two3)
+        part_a = one3 * wide(inv_n, 512)
+        part_b = two3 * wide(inv_n, 512)
+
+        def d_row(r, carry):
+            q = lax.div(r, 2)
+            here = pl.ds(pl.multiple_of(lax.rem(r, 2) * 128, 128), 128)
+            z = (v34[layer, q, here, :] - mean3) * inv3
+            dv = wide(pmask[q, here, :], 512) * scale3 * (g[q, here, :] - part_a - z * part_b)
+            put_shifted(1 + r, dv, True)
+            return carry
+
+        lax.fori_loop(0, ROWS, d_row, 0)
+        halo_start()
+
+        def grad_out(h, carry):
+            def get(q):
+                dg = shifted[pl.ds(1 + 2 * q, 2), :, 512 + CL : 1024].reshape(256, CG)
+                dt = dot_nt(dg, w_e[layer])
+                u[q] = dt
+                return dt.astype(BF16)
+
+            width_out(0, h, tg, get)
+            return carry
+
+        lax.fori_loop(0, 2, grad_out, 0)
+        swap_start(0)
+        halo_wait(True)
+
+        @pl.when(step > 0)
+        def _():
+            gw_copy(layer + 1).wait()
+
+        def conv_back(c, carry):
+            d_loc = jnp.zeros((256, 128), F32)
+            d_glo = jnp.zeros((256, 384), F32)
+            for i in range(3):
+                for j in range(3):
+                    rows = pl.ds(2 * c + 2 - i, 2)
+                    dd = shifted[rows, :, j * 512 : (j + 1) * 512].reshape(256, 512)
+                    d_loc = d_loc + dot_nt(dd, w_c[layer, 3 * i + j])
+                    d_glo = d_glo + dot_nt(dd[:, :CL], w_gl[layer, 3 * i + j])
+            g[c, :, 0:CL] = d_loc
+            g[c, :, CL:] = d_glo
+            return carry
+
+        lax.fori_loop(0, PAIRS, conv_back, 0)
+        swap_wait(0)
+
+        def put(f, y):
+            e2[f * 128 : (f + 1) * 128, :] = y
+
+        rows_forward_into(0, put)
+        mean2, inv2, gain2, bias2 = affine(layer, 1, FULL)
+        scale2 = gain2 * inv2
+        shift2 = bias2 - mean2 * scale2
+
+        def slope_block(f, sums):
+            rows = pl.ds(pl.multiple_of(f * 128, 128), 128)
+            v = mixed[layer, rows, :]
+            pre = v * scale2 + shift2
+            sg = sigmoid(pre)
+            e = e2[rows, :] * wide(qmask[rows, :], FULL) * (sg * (1.0 + pre * (1.0 - sg)))
+            e2[rows, :] = e
+            return sums[0] + fold(e), sums[1] + fold(e * ((v - mean2) * inv2))
+
+        put_sums(1, *lax.fori_loop(0, 5, slope_block, (zero_of(FULL), zero_of(FULL))))
+        sums_start(1)
+
+        for i in range(3):
+            def lift_grad(i=i):
+                acc = jnp.zeros((128, 1152), F32)
+                for q in range(PAIRS):
+                    rows = slice(2 * q + 2 - i, 2 * q + 4 - i)
+                    dd = jnp.concatenate(
+                        [shifted[rows, :, j * 512 + CL : (j + 1) * 512].reshape(256, CG) for j in range(3)], axis=1
+                    )
+                    acc = acc + dot(at[0:CL, q * 256 : (q + 1) * 256], dd)
+                for n in range(9):
+                    base = AT_KG + (9 * i + n) * 128
+                    gw[base : base + 128, :] = acc[:, n * 128 : (n + 1) * 128].astype(BF16)
+            lift_grad()
+        one2, two2 = sums_wait(1, FULL)
+        keep_grad_sums(layer, 1, FULL, one2, two2)
+        part_a2 = one2 * wide(inv_ns, FULL)
+        part_b2 = two2 * wide(inv_ns, FULL)
+
+        def dq_block(f, carry):
+            rows = pl.ds(pl.multiple_of(f * 128, 128), 128)
+            z = (mixed[layer, rows, :] - mean2) * inv2
+            dv = wide(qmask[rows, :], FULL) * scale2 * (e2[rows, :] - part_a2 - z * part_b2)
+            low_dv = dv.astype(BF16)
+            dq[rows, :] = low_dv
+            e2[rows, :] = dot_nt(low_dv, w_m[layer])
+            return carry
+
+        lax.fori_loop(0, 5, dq_block, 0)
+        rows_inverse_from(1, lambda f: e2[f * 128 : (f + 1) * 128, :])
+        swap_start(1)
+
+        def local_grad(c, carry):
+            for i in range(3):
+                acc = jnp.zeros((128, 384), F32)
+                for q in range(PAIRS):
+                    rows = slice(2 * q + 2 - i, 2 * q + 4 - i)
+                    dd = jnp.concatenate(
+                        [shifted[rows, :, j * 512 : j * 512 + CL].reshape(256, CL) for j in range(3)], axis=1
+                    )
+                    acc = acc + dot(at[pl.ds(pl.multiple_of(c * 128, 128), 128), q * 256 : (q + 1) * 256], dd)
+                for j in range(3):
+                    base = pl.multiple_of(AT_KL + (3 * i + j) * 512 + c * 128, 128)
+                    gw[pl.ds(base, 128), :] = acc[:, j * 128 : (j + 1) * 128].astype(BF16)
+            return carry
+
+        lax.fori_loop(0, 4, local_grad, 0)
+        acc_e = jnp.zeros((HALF, CG), F32)
+        for q in range(PAIRS):
+            dg = shifted[1 + 2 * q : 3 + 2 * q, :, 512 + CL : 1024].reshape(256, CG)
+            acc_e = acc_e + dot_tn(tsum[layer, q], dg)
+        for n in range(3):
+            gw[AT_E + n * HALF : AT_E + (n + 1) * HALF, :] = acc_e[:, n * 128 : (n + 1) * 128].astype(BF16)
+        acc_m = jnp.zeros((FULL, FULL), F32)
+        for f in range(5):
+            rows = slice(f * 128, (f + 1) * 128)
+            acc_m = acc_m + dot_tn(spec[layer, rows, :], dq[rows, :])
+        for n in range(3):
+            gw[AT_M + n * FULL : AT_M + (n + 1) * FULL, :] = acc_m[:, n * 128 : (n + 1) * 128].astype(BF16)
+        swap_wait(1)
+
+        mean1, inv1, gain1, bias1 = affine(layer, 0, HALF)
+        scale1 = gain1 * inv1
+        shift1 = bias1 - mean1 * scale1
+
+        def slope_in(h, sums):
+            backs = width_back(1, h, tft)
+            one, two = sums
+            for o in range(2):
+                q = 2 * h + o
+                v = v1[layer, q]
+                pre = v * scale1 + shift1
+                sg = sigmoid(pre)
+                e = (u[q] + backs[o]) * wide(pmask[q], HALF) * (sg * (1.0 + pre * (1.0 - sg)))
+                u[q] = e
+                one = one + fold(e)
+                two = two + fold(e * ((v - mean1) * inv1))
+            return one, two
+
+        put_sums(0, *lax.fori_loop(0, 2, slope_in, (zero_of(HALF), zero_of(HALF))))
+        sums_start(0)
+        one1, two1 = sums_wait(0, HALF)
+        keep_grad_sums(layer, 0, HALF, one1, two1)
+        part_a1 = one1 * wide(inv_n, HALF)
+        part_b1 = two1 * wide(inv_n, HALF)
+
+        def ds_pair(q, carry):
+            z = (v1[layer, q] - mean1) * inv1
+            dv = wide(pmask[q], HALF) * scale1 * (u[q] - part_a1 - z * part_b1)
+            low_dv = dv.astype(BF16)
+            ds[q] = low_dv
+            g[q, :, CL:] = g[q, :, CL:] + dot_nt(low_dv, w_r[layer])
+            return carry
+
+        lax.fori_loop(0, PAIRS, ds_pair, 0)
+        acc_r = jnp.zeros((CG, HALF), F32)
+        for q in range(PAIRS):
+            acc_r = acc_r + dot(at[CL:, q * 256 : (q + 1) * 256], ds[q])
+        gw[AT_R : AT_R + CG, :] = acc_r[:, 0:128].astype(BF16)
+        gw[AT_R + CG : AT_R + 2 * CG, 0:64] = acc_r[:, 128:HALF].astype(BF16)
+        gw_copy(layer).start()
+
+        @pl.when(lax.rem(layer, 2) == 0)
+        def _():
+            block = lax.div(layer, 2)
+
+            def close_row(r, carry):
+                q = lax.div(r, 2)
+                here = pl.ds(pl.multiple_of(lax.rem(r, 2) * 128, 128), 128)
+                x = (gblk[block, r].astype(F32) + g[q, here, :]) * wide(pmask[q, here, :], 512)
+                low_x = x.astype(BF16)
+                gblk[2 * block, r] = low_x
+
+                @pl.when(block == 1)
+                def _():
+                    gblk[0, r] = low_x
+                    g[q, here, :] = low_x.astype(F32)
+
+                return carry
+
+            lax.fori_loop(0, ROWS, close_row, 0)
+            start_out(g_copy(block))
+
+        return carry
+
+    gw[AT_R + CG : AT_R + 2 * CG, :] = jnp.zeros((CG, 128), BF16)
+    lax.fori_loop(0, LAYERS, backward, 0)
+
+    far = pltpu.make_async_remote_copy(
+        stats, stats_far, sem_st.at[0], sem_st.at[1],
+        device_id=(s, lax.rem(d + per, n_dp)), device_id_type=MESH,
+    )
+    far.start()
+    for block in range(2):
+        wait_out(y_copy(block))
+        wait_out(g_copy(block))
+    for m in range(2):
+        from_self = (lax.rem(d, 2) == s) & (m * per + lax.div(d, 2) == d)
+
+        @pl.when(jnp.logical_not(from_self))
+        def _(m=m):
+            pltpu.make_async_remote_copy(
+                acts.at[0], out_y.at[m], sem_y_s.at[0], sem_y_r.at[m], device_id=partner, device_id_type=MESH
+            ).wait_recv()
+            pltpu.make_async_remote_copy(
+                gblk.at[0], out_g.at[m], sem_g_s.at[0], sem_g_r.at[m], device_id=partner, device_id_type=MESH
+            ).wait_recv()
+
+    gw_copy(0).wait()
+    far.wait()
+    for lay in range(2):
+        mine = stats[2 * s + lay]
+        other = stats_far[2 * s + lay]
+        zero_first = jnp.where(grp == 0, mine, other)
+        one_next = jnp.where(grp == 0, other, mine)
+        for which, (lanes, at_count) in enumerate(((HALF, 2), (FULL, 4), (512, 2))):
+            mean = run[lay, which : which + 1, :]
+            var = run[lay, 3 + which : 4 + which, :]
+            for m, st in enumerate((zero_first, one_next)):
+                mean = (1.0 - MOMENTUM) * mean + MOMENTUM * st[which : which + 1]
+                fix = wide(counts[at_count + m : at_count + m + 1, :], 512)
+                var = (1.0 - MOMENTUM) * var + MOMENTUM * st[6 + which : 7 + which] * fix
+            out_p[lay, which : which + 1, :] = mean
+            out_p[lay, 3 + which : 4 + which, :] = var
+            for base in (9, 12):
+                total_sum = zero_first[base + which : base + which + 1] + one_next[base + which : base + which + 1]
+                out_p[lay, base - 3 + which : base - 2 + which, :] = total_sum
+        out_p[lay, 12:16, :] = jnp.zeros((4, 512), F32)
+
+
+def spectral_tables(height, width):
+    part = lax.broadcasted_iota(jnp.int32, (6, LONG, LONG), 0)
+    row = lax.broadcasted_iota(jnp.int32, (6, LONG, LONG), 1)
+    col = lax.broadcasted_iota(jnp.int32, (6, LONG, LONG), 2)
+    odd = part % 2 == 1
+    tall = part < 2
+    lifted = odd & ~tall & (row == 0)
+    index = jnp.where(lifted, LONG // 2, row)
+    side = jnp.where(tall, height, width)
+    phase = (index * col) % side
+    side_real = side.astype(jnp.float32)
+    angle = 2.0 * jnp.pi / side_real * phase.astype(jnp.float32)
+    wave = jnp.where(odd & ~lifted, jnp.where(tall, 1.0, -1.0) * jnp.sin(angle), jnp.cos(angle))
+    valid = (col < side) & (index < jnp.where(tall, height, width // 2 + 1))
+    edge = (index == 0) | (index == width // 2)
+    weight = jnp.where((part >= 4) & ~edge, 2.0, 1.0)
+    return jnp.where(valid, wave * weight * lax.rsqrt(side_real), 0.0)
+
+
+def pack_norms(array):
+    return jnp.stack(
+        [
+            jnp.pad(array[:, :CS], ((0, 0), (0, 512 - CS))),
+            jnp.pad(array[:, CS : 3 * CS], ((0, 0), (0, 512 - 2 * CS))),
+            array[:, 3 * CS :],
+        ],
+        axis=1,
+    )
+
+
+def unpack_norms(array):
+    return jnp.concatenate([array[:, 0, :CS], array[:, 1, : 2 * CS], array[:, 2]], axis=1)
+
+
+def tiles_of(rows, lanes, array):
+    return jnp.swapaxes(array.reshape(2, lanes // 128, rows, 128), 1, 2).reshape(2, rows, lanes)
+
+
+def on_band(
+    inputs,
+    cotangent,
+    shapes,
+    local_to_local,
+    global_to_local,
+    local_to_global,
+    spec_reduce,
+    spec_mix,
+    spec_expand,
+    norm_gains,
+    norm_biases,
+    run_means,
+    run_vars,
+):
+    section_id = lax.axis_index("section")
+    n_dp = lax.axis_size("dp")
+    group = lax.axis_index("dp") // (n_dp // 2)
+    own_shape = lax.dynamic_index_in_dim(shapes, group, 0, keepdims=False)
+    tables = spectral_tables(own_shape[0], own_shape[1])
+    zeros = jnp.zeros((2, 2, 512), jnp.float32)
+    pars = jnp.concatenate([pack_norms(norm_gains[0]), pack_norms(norm_biases[0]), zeros], axis=1)
+    run = jnp.concatenate([pack_norms(run_means[0]), pack_norms(run_vars[0]), zeros], axis=1)
+    pixels = (shapes[:, 0] * shapes[:, 1]).astype(jnp.float32)
+    points = (shapes[:, 0] * (shapes[:, 1] // 2 + 1)).astype(jnp.float32)
+    own_pixels = lax.dynamic_index_in_dim(pixels, group, 0)
+    own_points = lax.dynamic_index_in_dim(points, group, 0)
+    counts = jnp.concatenate(
+        [1.0 / own_pixels, 1.0 / own_points, pixels / (pixels - 1.0), points / (points - 1.0), jnp.zeros((2,))]
+    )
+    counts = jnp.broadcast_to(counts[:, None], (8, 128)).astype(jnp.float32)
+    anywhere = pl.BlockSpec(memory_space=pl.ANY)
+    vmem = pl.BlockSpec(memory_space=pltpu.VMEM)
+    dma = pltpu.SemaphoreType.DMA
+    band = (ROWS, LONG, 512)
+    out_y, out_g, out_w, out_p = pl.pallas_call(
+        network_kernel,
+        out_shape=(
+            jax.ShapeDtypeStruct((2,) + band, BF16),
+            jax.ShapeDtypeStruct((2,) + band, BF16),
+            jax.ShapeDtypeStruct((LAYERS, GRAD_ROWS, 128), BF16),
+            jax.ShapeDtypeStruct((2, 16, 512), F32),
+        ),
+        in_specs=[anywhere, anywhere, pl.BlockSpec(memory_space=pltpu.SMEM)]
+        + [anywhere] * 7
+        + [vmem] * 3,
+        out_specs=(anywhere, anywhere, anywhere, vmem),
+        scratch_shapes=[
+            pltpu.VMEM((LAYERS, 9, CL, 512), BF16),
+            pltpu.VMEM((LAYERS, 9, CG, CL), BF16),
+            pltpu.VMEM((LAYERS, CG, CS), BF16),
+            pltpu.VMEM((LAYERS, FULL, FULL), BF16),
+            pltpu.VMEM((LAYERS, CS, CG), BF16),
+            pltpu.VMEM((LAYERS, 8, 512), F32),
+            pltpu.VMEM((LAYERS + 1,) + band, BF16),
+            pltpu.VMEM((ROWS + 2, LONG, 1536), BF16),
+            pltpu.VMEM((2, LONG, 512), BF16),
+            pltpu.VMEM((LAYERS, PAIRS, 256, CS), F32),
+            pltpu.VMEM((PAIRS, 256, CS), F32),
+            pltpu.VMEM((LAYERS, SLOTS, FULL), BF16),
+            pltpu.VMEM((LAYERS, SLOTS, FULL), F32),
+            pltpu.VMEM((LAYERS, PAIRS, 256, CS), BF16),
+            pltpu.VMEM((LAYERS, PAIRS, 256, 512), F32),
+            pltpu.VMEM((PAIRS, 256, 128), F32),
+            pltpu.VMEM((SLOTS, 128), F32),
+            pltpu.VMEM((256, 256), BF16),
+            pltpu.VMEM((256, 256), BF16),
+            pltpu.VMEM((256, 256), BF16),
+            pltpu.VMEM((256, 256), BF16),
+            pltpu.VMEM((4, 256, 512), BF16),
+            pltpu.VMEM((512, 1024), BF16),
+            pltpu.VMEM((1024, FULL), BF16),
+            pltpu.VMEM((SLOTS, FULL), F32),
+            pltpu.VMEM((SLOTS, FULL), BF16),
+            pltpu.VMEM((PAIRS, 256, CS), BF16),
+            pltpu.VMEM((PAIRS, 256, 512), F32),
+            pltpu.VMEM((3,) + band, BF16),
+            pltpu.VMEM((512, ROWS * LONG), BF16),
+            pltpu.VMEM((GRAD_ROWS, 128), BF16),
+            pltpu.VMEM((4, 8, 128), F32),
+            pltpu.VMEM((4, MEMBERS, 8, 128), F32),
+            pltpu.VMEM((2, MEMBERS, 32, FULL), BF16),
+            pltpu.VMEM((2, MEMBERS, 32, FULL), BF16),
+            pltpu.VMEM((LAYERS, 16, 512), F32),
+            pltpu.VMEM((LAYERS, 16, 512), F32),
+            dma((3, 8)),
+            dma((2,)),
+            dma((2,)),
+            dma((2,)),
+            dma((2,)),
+            dma((4, MEMBERS)),
+            dma((4, MEMBERS)),
+            dma((2, MEMBERS)),
+            dma((2, MEMBERS)),
+            dma((2,)),
+            dma((2,)),
+            dma((2,)),
+            dma((2,)),
+            dma,
+            dma((2,)),
+        ],
+        compiler_params=pltpu.CompilerParams(
+            collective_id=0, has_side_effects=True, vmem_limit_bytes=63 << 20
+        ),
+        name="network",
+    )(
+        inputs[:, 0],
+        cotangent[:, 0],
+        shapes,
+        local_to_local[0],
+        global_to_local[0],
+        local_to_global[0],
+        spec_reduce[0],
+        spec_mix[0],
+        spec_expand[0],
+        pars,
+        run,
+        tables,
+        counts,
+    )
+    sent = lax.dynamic_slice_in_dim(out_w, 2 * (1 - section_id), 2, 0)
+    kept = lax.dynamic_slice_in_dim(out_w, 2 * section_id, 2, 0)
+    other = lax.ppermute(sent, "section", [(0, 1), (1, 0)])
+    totals = lax.psum(kept.astype(F32) + other.astype(F32), "dp")
+    grad_local = totals[:, AT_KL:AT_KG].reshape(2, 9, 512, 128)
+    grad_lift = totals[:, AT_KG:AT_E].reshape(2, 9, 3, 128, 128)
+    grad_lift = jnp.swapaxes(grad_lift, 2, 3).reshape(2, 9, CL, CG)
+    grad_expand = tiles_of(CS, CG, totals[:, AT_E : AT_E + 3 * CS])
+    grad_mix = tiles_of(FULL, FULL, totals[:, AT_M : AT_M + 3 * FULL])
+    grad_reduce = tiles_of(CG, 256, totals[:, AT_R : AT_R + 2 * CG])[..., :CS]
+    return (
+        out_y[None, :, None],
+        out_g.astype(F32)[None, :, None],
+        grad_local[None, :, :, :CL],
+        grad_local[None, :, :, CL:],
+        grad_lift[None],
+        grad_reduce[None],
+        grad_mix[None],
+        grad_expand[None],
+        unpack_norms(out_p[:, 9:12])[None],
+        unpack_norms(out_p[:, 6:9])[None],
+        unpack_norms(out_p[:, 0:3])[None],
+        unpack_norms(out_p[:, 3:6])[None],
+    )
+
+
 def solution(mesh):
     in_specs = (
         P(None, None, "dp", None, None),
@@ -554,6 +1569,8 @@
         P("section", None, None),
         P("section", None, None),
     )
+    dp_size = mesh.shape["dp"]
+    banded = dp_size == MEMBERS and LONG == dp_size * ROWS
     return jax.shard_map(
-        on_device, mesh=mesh, in_specs=in_specs, out_specs=out_specs, check_vma=False
-    )
+        on_band if banded else on_device, mesh=mesh, in_specs=in_specs, out_specs=out_specs, check_vma=False
+    )

time: 2880 us -> 874 us (0.30)
  blocking collectives: 1440 us -> 0 us
  Pallas kernels: 0 us -> 465 us
  matrix products: 431 us -> 0 us
  local copies, waits for them, and re-layouts: 266 us -> 45.1 us
  other arithmetic: 211 us -> 22.9 us
  starting transfers between devices: 185 us -> 0.04 us
  waiting for transfers between devices: 276 us -> 322 us
  between operations: 49.8 us -> 18.3 us
    psum x36 -> x0, blocking collectives: 1440 us -> none  [the longest x18 729 us: moments(): totals = lax.psum(jnp.concatenate(pieces), 'dp')]
    pallas_call x0 -> x1, Pallas kernels: none -> 465 us  [on_band(): pl.pallas_call(network_kernel, out_shape=(jax.ShapeDtypeStruct((2,) + ban...]
    dot_general x306 -> x0, matrix products: 367 us -> none  [the longest x108 87.1 us: kernel_grad(): jnp.einsum('mrwi,mrwo->io', window, grad_out, preferred_element_type=jnp....]
    all_to_all x24 -> x0, starting transfers between devices: 103 us -> none  [the longest x6 27.5 us: layer_forward(): lax.all_to_all(inverse, 'dp', split_axis=1, concat_axis=2, tiled=True)]
    ppermute x28 -> x1, starting transfers between devices: 81.6 us -> 0.01 us  [on_band(): other = lax.ppermute(sent, 'section', [(0, 1), (1, 0)])]
    conv_general_dilated x120 -> x0, local copies, waits for them, and re-layouts: 79.4 us -> none  [conv_rows(): lax.conv_general_dilated(padded, shaped, (1, 1), 'VALID', dimension_numbe...]
    conv_general_dilated x24 -> x0, matrix products: 63.2 us -> none  [conv_rows(): lax.conv_general_dilated(padded, shaped, (1, 1), 'VALID', dimension_numbe...]
    unnamed x1108 -> x16, local copies, waits for them, and re-layouts: 70.5 us -> 9.63 us
  transfers between devices with their start and end apart: 53 -> 2, of which waited for: 12 -> 2; matrix products, arithmetic and copies ran while one was open for 12% -> 1% of each run, Pallas kernels for 0% -> 0%
where the time goes in v1:
time: 874 us; the launch traced here: 873 us
  Pallas kernels  465 us (53%)
  waiting for transfers between devices  322 us (37%)
  local copies, waits for them, and re-layouts  45.1 us (5%)
  other arithmetic  22.9 us (3%)
  between operations  18.3 us (2%)
    pallas_call x1, Pallas kernels, on_band(): pl.pallas_call(network_kernel, out_shape=(jax.ShapeDtypeStruct((2,) + ban...  465 us
    psum x1, waiting for transfers between devices, on_band(): totals = lax.psum(kept.astype(F32) + other.astype(F32), 'dp')  312 us
  transfers between devices with their start and end apart: 2, of which 2 were waited for; matrix products, arithmetic and copies ran while one was open for 1% of the time, Pallas kernels for 0%

profile of v1, /device:TPU:0, one launch (start us, length us, event | category | flops | bytes accessed | tf_op | source)
XLA Modules:
  0.0 872.7 jit_solution(3797630403268647925)
XLA Ops:
  11.2 1.0 slice_reduce_fusion
  12.1 0.8 slice.175
  12.9 0.8 slice.178
  13.6 0.8 slice_bitcast_fusion.3
  14.5 0.8 slice_bitcast_fusion.5
  15.3 0.8 slice.169
  16.0 0.8 fusion.27
  16.8 0.8 slice.172
  17.6 1.3 broadcast_compare_fusion
  22.3 1.9 copy.51
  25.6 6.4 multiply_select_fusion.tables
  32.7 464.8 %network.1 = (bf16[2,8,128,512]{3,2,1,0:T(8,128)(2,1)}, bf16[2,8,128,512]{3,2,1,0:T(8,128)(2,1)}, bf16[4,10752,128]{2,1,0:T(8,128)(2,1)}, f32[2,16,512]{2,1,0:T(8,128)}) custom-call(bf16[2,8,128,512]{3,2,1,0:T(8,128)(2,1)} %bitcast.110, bf16[2,8,128,512]{3,2,1,0:T(8,128)(2,1)} %bitcast.111, s32[2,2]{1,0:T(2,128)} %shapes.1, ...), custom_call_target="tpu_custom_call" | custom-call | tf_op jit(solution)/shard_map/network/pallas_call | solution.py:1431
  497.5 5.9 constant_dynamic-slice_fusion
  503.4 9.4 %collective-permute-done = bf16[2,10752,128]{2,1,0:T(8,128)(2,1)} collective-permute-done((bf16[2,10752,128]{2,1,0:T(8,128)(2,1)}, bf16[2,10752,128]{2,1,0:T(8,128)(2,1)}, u32[]{:S(2)}, u32[]{:S(2)}) %collective-permute-start) | collective-permute-done | bytes 5505056 | tf_op jit(solution)/shard_map/ppermute | solution.py:1518
  512.8 9.5 %convert_add_fusion = f32[2,10752,128]{2,1,0:T(8,128)} fusion(bf16[2,10752,128]{2,1,0:T(8,128)(2,1)} %collective-permute-done, bf16[4,10752,128]{2,1,0:T(8,128)(2,1)} %get-tuple-element.18, s32[]{:T(128)S(6)} %select_n.99), kind=kLoop, calls=%fused_computation | loop fusion | flops 8257536 | bytes 22020100 | tf_op jit(solution)/shard_map/add | solution.py:1519
  522.4 0.8 copy-done.3
  523.4 0.7 concatenate.24
  526.1 2.6 bitcast_convert_fusion
  528.7 312.1 %all-reduce.6.cloned.1.call-done = f32[2,10752,128]{2,1,0:T(8,128)} async-done(((f32[2,10752,128]{2,1,0:T(8,128)}), f32[2,10752,128]{2,1,0:T(8,128)}) %all-reduce.6.cloned.1.call-update) | async-done | bytes 11010064 | tf_op jit(solution)/shard_map/psum | solution.py:1519
  840.8 2.8 slice.180
  843.6 2.1 slice_bitcast_fusion
  845.8 1.1 slice_bitcast_fusion.1
  846.9 1.2 copy-done
  848.1 2.0 slice.183
  850.1 3.3 copy.63
  853.4 2.9 copy.77
  856.4 2.4 slice.186
  858.8 1.6 copy.65
  860.5 1.4 copy.78
  862.1 0.9 slice_bitcast_fusion.2
  863.4 1.1 broadcast_in_dim_reshape.11
  864.6 1.3 copy.95
  (59 shorter events, 8.3 us)
Async XLA Ops:
  7.2 833.7 %all-reduce.6.cloned.1.call-start = ((), (), s32[]{:S(2)}) async-start(), calls=%async_computation | async-start | bytes 22020096 | tf_op jit(solution)/shard_map/psum | solution.py:1519
  503.4 9.4 %collective-permute-start = (bf16[2,10752,128]{2,1,0:T(8,128)(2,1)}, bf16[2,10752,128]{2,1,0:T(8,128)(2,1)}, u32[]{:S(2)}, u32[]{:S(2)}) collective-permute-start(bf16[2,10752,128]{2,1,0:T(8,128)(2,1)} %constant_dynamic-slice_fusion), channel_id=1, source_target_pairs={{0,16},{16,0},{1,17},{17,1},{2,18},{18,2},{3,19},{19,3},{4,20},{20... | collective-permute-start | bytes 16515080 | tf_op jit(solution)/shard_map/ppermute | solution.py:1518
  522.4 0.8 copy-start.3
  522.4 3.8 copy-start.1
  840.8 7.3 copy-start
  856.4 5.5 slice-start
  860.5 2.5 slice-start.1
  863.0 1.6 copy-start.2
Sparse Core Ops, SparseCore 0:
  522.5 318.2 all-reduce.5
